TPU v7x, 32 devices: a whole 2x2x4 slice. The times are simulated.
32 devices in a mesh: seq: 8 (over z, y), shard: 4 (over x, core).
Axes of the slice: x: 2, y: 2, z: 4, core: 2. Of those that a mesh axis runs over, the one named last changes fastest.
Arguments:
- block_input: bfloat16 [8, 4096, 640], P('shard', 'seq'), may hold values from -6 to 6
- out_grad: bfloat16 [8, 4096, 640], P('shard', 'seq'), may hold values from -6 to 6
- positions: int32 [8, 4096], P('shard', 'seq'), may hold values from 0 to 6142, as said below
- segments: int32 [8, 4096], P('shard', 'seq'), may hold values from 0 to 4, as said below
- qkv_weight: float32 [640, 1536], P(None, 'shard'), may hold values from -0.25 to 0.25
- out_weight: float32 [1024, 640], P('shard'), may hold values from -0.1875 to 0.1875
- ff_in_weight: float32 [2, 640, 2048], P(None, None, 'shard'), may hold values from -0.25 to 0.25
- ff_out_weight: float32 [2048, 640], P('shard'), may hold values from -0.125 to 0.125
- norm_gains: float32 [3072], P('shard'), may hold values from 0.5 to 1.5
- qkv_moment: float32 [640, 1536], P(None, 'shard'), as said below
- qkv_square: float32 [640, 1536], P(None, 'shard'), may hold values from 1724 to 6898
- out_moment: float32 [1024, 640], P('shard'), as said below
- out_square: float32 [1024, 640], P('shard'), may hold values from 1724 to 6898
- ff_in_moment: float32 [2, 640, 2048], P(None, None, 'shard'), as said below
- ff_in_square: float32 [2, 640, 2048], P(None, None, 'shard'), may hold values from 1724 to 6898
- ff_out_moment: float32 [2048, 640], P('shard'), as said below
- ff_out_square: float32 [2048, 640], P('shard'), may hold values from 1724 to 6898
- gains_moment: float32 [3072], P('shard'), as said below
- gains_square: float32 [3072], P('shard'), may hold values from 1724 to 6898
Outputs:
- mixed: bfloat16 [8, 4096, 640], P('shard', 'seq')
- input_grad: bfloat16 [8, 4096, 640], P('shard', 'seq')
- qkv_updated: float32 [640, 1536], P(None, 'shard')
- qkv_moment_new: float32 [640, 1536], P(None, 'shard')
- qkv_square_new: float32 [640, 1536], P(None, 'shard')
- out_updated: float32 [1024, 640], P('shard')
- out_moment_new: float32 [1024, 640], P('shard')
- out_square_new: float32 [1024, 640], P('shard')
- ff_in_updated: float32 [2, 640, 2048], P(None, None, 'shard')
- ff_in_moment_new: float32 [2, 640, 2048], P(None, None, 'shard')
- ff_in_square_new: float32 [2, 640, 2048], P(None, None, 'shard')
- ff_out_updated: float32 [2048, 640], P('shard')
- ff_out_moment_new: float32 [2048, 640], P('shard')
- ff_out_square_new: float32 [2048, 640], P('shard')
- gains_updated: float32 [3072], P('shard')
- gains_moment_new: float32 [3072], P('shard')
- gains_square_new: float32 [3072], P('shard')
Inputs may be any that keep to these rules, and one draw needn't show every extreme that they name: `segments`: within each sequence the ids start at 0 and never fall; in each aligned group of 2 sequences one sequence is a single document, and every other sequence has exactly 5 documents. `positions`: A token's position is its document's first position plus its distance from the document's first token; each document's first position is below 2048. `qkv_moment`: entries of mean zero with a deviation of 0.111 times the square root of 32768. `out_moment`: entries of mean zero with a deviation of 0.111 times the square root of 32768. `ff_in_moment`: entries of mean zero with a deviation of 0.111 times the square root of 32768. `ff_out_moment`: entries of mean zero with a deviation of 0.111 times the square root of 32768. `gains_moment`: entries of mean zero with a deviation of 0.111 times the square root of 32768.
All inputs are finite; a program needn't handle non-finite values.
Results may differ from a plain program's by a relative error of at most 0.02.
The roundings to bfloat16 on the way count: a program that leaves them out, or rounds other values in their place, can miss the bound.
Values may be sent and summed in bfloat16 or wider, within the bound.
A program may use at most 192 MiB of HBM per device.

v0:
```python
from functools import partial

import jax
import jax.numpy as jnp
from jax import lax
from jax.sharding import PartitionSpec as P

D = 640
QH = 4
HEAD = 256
WINDOW = 512
STEP = 10


eps_norm = 1e-06
rope_base = 10000.0
beta_first = 0.9
beta_second = 0.95
adam_eps = 1e-08
rate_matrix = 0.05
rate_gain = 0.8
decay_matrix = 0.1
masked_score = -1e30


def from_behind(block, axis, distance):
    devices = range(lax.axis_size(axis))
    route = [(i - distance, i) for i in devices if i - distance in devices]
    return lax.ppermute(block, axis, route)


def rms_scale(values, scales):
    return values * lax.rsqrt(jnp.mean(values * values, axis=-1, keepdims=True) + eps_norm) * scales


def rope_tables(positions):
    freqs = 1.0 / rope_base ** (jnp.arange(0, HEAD, 2, dtype=jnp.float32) / HEAD)
    angles = positions.astype(jnp.float32)[..., None] * freqs
    return (jnp.cos(angles), jnp.sin(angles))


def rotate(values, cos_table, sine_table):
    half_width = values.shape[-1] // 2
    first_half = values[..., :half_width]
    second_half = values[..., half_width:]
    return jnp.concatenate(
        [
            first_half * cos_table - second_half * sine_table,
            second_half * cos_table + first_half * sine_table,
        ],
        axis=-1,
    )


def split_gains(gain_all):
    return (
        gain_all[0:D],
        gain_all[D : 2 * D],
        gain_all[2 * D : 3 * D],
        gain_all[3 * D : 4 * D],
        gain_all[4 * D : 4 * D + HEAD],
        gain_all[4 * D + HEAD : 4 * D + 2 * HEAD],
    )


def head_post(project, gain_query, gain_key, cos_table, sine_table):
    queries = project[..., : QH * HEAD].reshape(project.shape[:-1] + (QH, HEAD))
    key_rows = project[..., QH * HEAD : (QH + 1) * HEAD]
    value_rows = project[..., (QH + 1) * HEAD :]
    queries = rotate(
        rms_scale(queries, gain_query), cos_table[..., None, :], sine_table[..., None, :]
    )
    key_rows = rotate(rms_scale(key_rows, gain_key), cos_table, sine_table)
    return (queries, key_rows, value_rows)


def score_block(queries, key_rows, allowed):
    scores = jnp.einsum(
        "sqhd,skd->shqk", queries, key_rows, preferred_element_type=jnp.float32
    ) * HEAD ** (-0.5)
    return jnp.where(allowed[:, None], scores, masked_score)


def adam_step(weight, gradient, moment, square, step_rate, decay_rate):
    moment_new = beta_first * moment + (1.0 - beta_first) * gradient
    square_new = beta_second * square + (1.0 - beta_second) * gradient * gradient
    moment_hat = moment_new / (1.0 - beta_first**STEP)
    square_hat = square_new / (1.0 - beta_second**STEP)
    weight_new = weight - step_rate * (
        moment_hat / (jnp.sqrt(square_hat) + adam_eps) + decay_rate * weight
    )
    return (weight_new, moment_new, square_new)


def on_device(
    block_input,
    out_grad,
    positions,
    segments,
    qkv_weight,
    out_weight,
    ff_in_weight,
    ff_out_weight,
    norm_gains,
    qkv_moment,
    qkv_square,
    out_moment,
    out_square,
    ff_in_moment,
    ff_in_square,
    ff_out_moment,
    ff_out_square,
    gains_moment,
    gains_square,
):
    seqs_here, span_rows, model_width = block_input.shape
    row_count = seqs_here * span_rows
    w_qkv, w_out, w_ffin, w_ffout, gains_low = (
        lax.all_gather(qkv_weight.astype(jnp.bfloat16), "shard", axis=1, tiled=True),
        lax.all_gather(out_weight.astype(jnp.bfloat16), "shard", axis=0, tiled=True),
        lax.all_gather(ff_in_weight.astype(jnp.bfloat16), "shard", axis=2, tiled=True),
        lax.all_gather(ff_out_weight.astype(jnp.bfloat16), "shard", axis=0, tiled=True),
        lax.all_gather(norm_gains.astype(jnp.bfloat16), "shard", axis=0, tiled=True),
    )
    gain_in, gain_attn, gain_pre, gain_post, gain_query, gain_key = split_gains(
        gains_low.astype(jnp.float32)
    )
    tokens = block_input.astype(jnp.float32).reshape(row_count, model_width)
    normed = rms_scale(tokens, gain_in).astype(jnp.bfloat16)
    project = jnp.dot(normed, w_qkv, preferred_element_type=jnp.float32).reshape(
        seqs_here, span_rows, -1
    )
    cos_table, sine_table = rope_tables(positions)
    query_full, key_full, value_full = head_post(
        project, gain_query, gain_key, cos_table, sine_table
    )
    queries = query_full.astype(jnp.bfloat16)
    keys_own = key_full.astype(jnp.bfloat16)
    values_own = value_full.astype(jnp.bfloat16)
    key_prev, value_prev, segment_prev = from_behind((keys_own, values_own, segments), "seq", 1)
    is_first = lax.axis_index("seq") == 0
    distance = jnp.arange(span_rows)[:, None] - (jnp.arange(WINDOW + span_rows)[None, :] - WINDOW)
    in_window = (distance >= 0) & (distance < WINDOW)
    from_prev = (jnp.arange(WINDOW + span_rows) >= WINDOW) | jnp.logical_not(is_first)
    key_segments = jnp.concatenate([segment_prev, segments], axis=1)
    same_doc = segments[:, :, None] == key_segments[:, None, :]
    allowed = in_window[None] & from_prev[None, None, :] & same_doc
    all_keys = jnp.concatenate([key_prev, keys_own], axis=1)
    all_values = jnp.concatenate([value_prev, values_own], axis=1)
    scores = score_block(queries, all_keys, allowed)
    row_top = jnp.max(scores, axis=-1, keepdims=True)
    exp_terms = jnp.exp(scores - row_top)
    row_total = jnp.sum(exp_terms, axis=-1, keepdims=True)
    attn_probs = exp_terms / row_total
    log_total = row_top + jnp.log(row_total)
    attended = jnp.einsum(
        "shqk,skd->sqhd",
        attn_probs.astype(jnp.bfloat16),
        all_values,
        preferred_element_type=jnp.float32,
    )
    attended_low = attended.reshape(row_count, QH * HEAD).astype(jnp.bfloat16)
    branch = jnp.dot(attended_low, w_out, preferred_element_type=jnp.float32)
    middle = tokens + rms_scale(branch, gain_attn)
    normed_two = rms_scale(middle, gain_pre).astype(jnp.bfloat16)
    gate_proj = jnp.dot(normed_two, w_ffin[0], preferred_element_type=jnp.float32)
    upward = jnp.dot(normed_two, w_ffin[1], preferred_element_type=jnp.float32)
    hidden = (jax.nn.gelu(gate_proj, approximate=True) * upward).astype(jnp.bfloat16)
    branch_two = jnp.dot(hidden, w_ffout, preferred_element_type=jnp.float32)
    mixed = (
        (middle + rms_scale(branch_two, gain_post))
        .astype(jnp.bfloat16)
        .reshape(seqs_here, span_rows, model_width)
    )
    cotangent = out_grad.astype(jnp.float32).reshape(row_count, model_width)
    post_back = jax.vjp(rms_scale, branch_two, gain_post)[1]
    grad_branch_two, grad_gain_post = post_back(cotangent)
    grad_ffn_low = grad_branch_two.astype(jnp.bfloat16)
    grad_ffout = jnp.einsum("nf,nd->fd", hidden, grad_ffn_low, preferred_element_type=jnp.float32)
    grad_hidden = jnp.einsum("nd,fd->nf", grad_ffn_low, w_ffout, preferred_element_type=jnp.float32)
    gelu_back = jax.vjp(
        lambda gate_in, up_in: jax.nn.gelu(gate_in, approximate=True) * up_in, gate_proj, upward
    )[1]
    grad_gate, grad_up = gelu_back(grad_hidden)
    grad_gate_low = grad_gate.astype(jnp.bfloat16)
    grad_up_low = grad_up.astype(jnp.bfloat16)
    grad_ffin = jnp.stack(
        [
            jnp.einsum("nd,nf->df", normed_two, grad_gate_low, preferred_element_type=jnp.float32),
            jnp.einsum("nd,nf->df", normed_two, grad_up_low, preferred_element_type=jnp.float32),
        ]
    )
    grad_normed_two = jnp.einsum(
        "nf,df->nd", grad_gate_low, w_ffin[0], preferred_element_type=jnp.float32
    ) + jnp.einsum("nf,df->nd", grad_up_low, w_ffin[1], preferred_element_type=jnp.float32)
    pre_back = jax.vjp(rms_scale, middle, gain_pre)[1]
    grad_middle_ffn, grad_gain_pre = pre_back(grad_normed_two)
    grad_middle = cotangent + grad_middle_ffn
    attn_back = jax.vjp(rms_scale, branch, gain_attn)[1]
    grad_branch, grad_gain_attn = attn_back(grad_middle)
    grad_attn_low = grad_branch.astype(jnp.bfloat16)
    grad_out = jnp.einsum(
        "nk,nd->kd", attended_low, grad_attn_low, preferred_element_type=jnp.float32
    )
    grad_attended = jnp.einsum(
        "nd,kd->nk", grad_attn_low, w_out, preferred_element_type=jnp.float32
    )
    grad_attended = grad_attended.astype(jnp.bfloat16).reshape(seqs_here, span_rows, QH, HEAD)
    scores_back = score_block(queries, all_keys, allowed)
    probs_back = jnp.exp(scores_back - log_total)
    grad_values = jnp.einsum(
        "shqk,sqhd->skd",
        probs_back.astype(jnp.bfloat16),
        grad_attended,
        preferred_element_type=jnp.float32,
    )
    grad_probs = jnp.einsum(
        "sqhd,skd->shqk", grad_attended, all_values, preferred_element_type=jnp.float32
    )
    inner_sum = jnp.sum(probs_back * grad_probs, axis=-1, keepdims=True)
    grad_scores = (probs_back * (grad_probs - inner_sum)).astype(jnp.bfloat16)
    grad_queries = jnp.einsum(
        "shqk,skd->sqhd", grad_scores, all_keys, preferred_element_type=jnp.float32
    ) * HEAD ** (-0.5)
    grad_keys = jnp.einsum(
        "shqk,sqhd->skd", grad_scores, queries, preferred_element_type=jnp.float32
    ) * HEAD ** (-0.5)
    grad_key_next, grad_value_next = (
        from_behind(grad_keys[:, :WINDOW].astype(jnp.bfloat16), "seq", -1).astype(jnp.float32),
        from_behind(grad_values[:, :WINDOW].astype(jnp.bfloat16), "seq", -1).astype(jnp.float32),
    )
    grad_key_own = grad_keys[:, WINDOW:] + grad_key_next
    grad_value_own = grad_values[:, WINDOW:] + grad_value_next
    head_back = jax.vjp(
        partial(head_post, cos_table=cos_table, sine_table=sine_table),
        project,
        gain_query,
        gain_key,
    )[1]
    grad_project, grad_gain_query, grad_gain_key = head_back(
        (grad_queries, grad_key_own, grad_value_own)
    )
    grad_project_low = grad_project.reshape(row_count, -1).astype(jnp.bfloat16)
    grad_qkv = jnp.einsum("nd,nk->dk", normed, grad_project_low, preferred_element_type=jnp.float32)
    grad_normed = jnp.einsum(
        "nk,dk->nd", grad_project_low, w_qkv, preferred_element_type=jnp.float32
    )
    in_back = jax.vjp(rms_scale, tokens, gain_in)[1]
    grad_tokens, grad_gain_in = in_back(grad_normed)
    input_grad = (
        (grad_middle + grad_tokens).astype(jnp.bfloat16).reshape(seqs_here, span_rows, model_width)
    )
    grad_gains = jnp.concatenate(
        [
            grad_gain_in,
            grad_gain_attn,
            grad_gain_pre,
            grad_gain_post,
            grad_gain_query,
            grad_gain_key,
        ]
    )
    shard_grads = (
        lax.psum_scatter(
            grad_qkv.astype(jnp.bfloat16), "shard", scatter_dimension=1, tiled=True
        ).astype(jnp.float32),
        lax.psum_scatter(
            grad_out.astype(jnp.bfloat16), "shard", scatter_dimension=0, tiled=True
        ).astype(jnp.float32),
        lax.psum_scatter(
            grad_ffin.astype(jnp.bfloat16), "shard", scatter_dimension=2, tiled=True
        ).astype(jnp.float32),
        lax.psum_scatter(
            grad_ffout.astype(jnp.bfloat16), "shard", scatter_dimension=0, tiled=True
        ).astype(jnp.float32),
        lax.psum_scatter(
            grad_gains.astype(jnp.bfloat16), "shard", scatter_dimension=0, tiled=True
        ).astype(jnp.float32),
    )
    masters = (qkv_weight, out_weight, ff_in_weight, ff_out_weight, norm_gains)
    moments = (qkv_moment, out_moment, ff_in_moment, ff_out_moment, gains_moment)
    squares = (qkv_square, out_square, ff_in_square, ff_out_square, gains_square)
    step_rates = (rate_matrix, rate_matrix, rate_matrix, rate_matrix, rate_gain)
    decays = (decay_matrix, decay_matrix, decay_matrix, decay_matrix, 0.0)
    totals = lax.psum(
        (shard_grads[0], shard_grads[1], shard_grads[2], shard_grads[3], shard_grads[4]), "seq"
    )
    results = [
        adam_step(
            masters[weight_index],
            totals[weight_index],
            moments[weight_index],
            squares[weight_index],
            step_rates[weight_index],
            decays[weight_index],
        )
        for weight_index in range(5)
    ]
    return (
        mixed,
        input_grad,
        results[0][0],
        results[0][1],
        results[0][2],
        results[1][0],
        results[1][1],
        results[1][2],
        results[2][0],
        results[2][1],
        results[2][2],
        results[3][0],
        results[3][1],
        results[3][2],
        results[4][0],
        results[4][1],
        results[4][2],
    )


def solution(mesh):
    return jax.shard_map(
        on_device,
        mesh=mesh,
        in_specs=(
            P("shard", "seq", None),
            P("shard", "seq", None),
            P("shard", "seq"),
            P("shard", "seq"),
            P(None, "shard"),
            P("shard", None),
            P(None, None, "shard"),
            P("shard", None),
            P("shard"),
            P(None, "shard"),
            P(None, "shard"),
            P("shard", None),
            P("shard", None),
            P(None, None, "shard"),
            P(None, None, "shard"),
            P("shard", None),
            P("shard", None),
            P("shard"),
            P("shard"),
        ),
        out_specs=(
            P("shard", "seq", None),
            P("shard", "seq", None),
            P(None, "shard"),
            P(None, "shard"),
            P(None, "shard"),
            P("shard", None),
            P("shard", None),
            P("shard", None),
            P(None, None, "shard"),
            P(None, None, "shard"),
            P(None, None, "shard"),
            P("shard", None),
            P("shard", None),
            P("shard", None),
            P("shard"),
            P("shard"),
            P("shard"),
        ),
        check_vma=False,
    )
```

profile of v0, /device:TPU:0, one launch (start us, length us, event | category | flops | bytes accessed | tf_op | source)
XLA Modules:
  0.0 612.4 jit_solution(17974415311096414064)
XLA Ops:
  12.8 5.0 collective-permute-start.1
  20.2 5.2 all-gather
  29.1 5.7 all-gather.6.cloned.1.call-done
  54.1 5.7 reshape.291
  69.2 8.5 %fusion.95 = (f32[2,4,512]{2,1,0:T(4,128)S(1)}, f32[2,4,512,1024]{2,3,1,0:T(8,128)}) fusion(bf16[2,512,4,128]{3,1,2,0:T(8,128)(2,1)S(1)} %get-tuple-element.57, bf16[2,512,4,128]{3,1,2,0:T(8,128)(2,1)S(1)} %get-tuple-element.56, bf16[2,512,128]{2,1,0:T(8,128)(2,1)S(1)} %get-tuple-element.63, bf16[2,512,128]{2,1,0:T(8,128)(2,1)S(1)} %get-tuple-element.62, ...), kind=kOutput, calls=%fused_computation.192 | convolution fusion | flops 2167402496 | bytes 20987904 | tf_op jit(solution)/shard_map/sqhd,skd->shqk/dot_general | solution.py:78
  77.7 8.1 %fusion.3 = f32[2,4,512]{2,1,0:T(4,128)S(1)} fusion(f32[2,4,512,1024]{2,3,1,0:T(8,128)} %get-tuple-element.75, f32[2,4,512]{2,1,0:T(4,128)S(1)} %get-tuple-element.74), kind=kLoop, calls=%fused_computation.9 | loop fusion | flops 8384512 | bytes 16809984 | tf_op jit(solution)/shard_map/reduce_sum | solution.py:153
  85.8 10.6 %convert_bitcast_fusion = bf16[2,512,4,256]{1,3,2,0:T(8,128)(2,1)} fusion(f32[2,4,512,1024]{2,3,1,0:T(8,128)} %get-tuple-element.75, f32[2,4,512]{2,1,0:T(4,128)S(1)} %fusion.3, f32[2,4,512]{2,1,0:T(4,128)S(1)} %get-tuple-element.74, bf16[2,512,256]{2,1,0:T(8,128)(2,1)S(1)} %slice.130, bf16[2,512,256]{2,1,0:T(8,128)(2,1)} %collective-permute-done), kind=kOutput, calls=%fused_computation.96 | convolution fusion | flops 2163212288 | bytes 19955712 | tf_op jit(solution)/shard_map/shqk,skd->sqhd/dot_general | solution.py:156
  108.4 5.7 fusion.37
  117.4 7.7 %multiply_convert_fusion.1 = (bf16[1024,2048]{1,0:T(8,128)(2,1)}, f32[1024,2048]{1,0:T(8,128)}) fusion(f32[1024,2048]{1,0:T(8,128)S(1)} %fusion.37, bf16[1024,640]{1,0:T(8,128)(2,1)S(1)} %copy-done.27, bf16[2,640,2048]{2,1,0:T(8,128)(2,1)S(1)} %copy-done.65), kind=kOutput, calls=%fused_computation.23 | convolution fusion | flops 2705326080 | bytes 24903680 | tf_op jit(solution)/shard_map/dot_general | solution.py:167
  125.3 6.2 %multiply_reduce_fusion.6 = (f32[1024]{0:T(1024)S(1)}, f32[1024,640]{1,0:T(8,128)S(1)}) fusion(bf16[1024,2048]{1,0:T(8,128)(2,1)} %get-tuple-element.78, bf16[2048,640]{1,0:T(8,128)(2,1)} %all-gather.12.cloned.1.call-done), kind=kOutput, calls=%fused_computation.84 | convolution fusion | flops 2685664256 | bytes 9441280 | tf_op jit(solution)/shard_map/dot_general | solution.py:169
  134.9 13.5 %multiply_convert_fusion = (bf16[1024,2048]{1,0:T(8,128)(2,1)}, bf16[1024,2048]{1,0:T(8,128)(2,1)S(1)}) fusion(f32[1024,2048]{1,0:T(8,128)} %copy-done.69, f32[1024,2048]{1,0:T(8,128)} %get-tuple-element.79, bf16[1024,640]{1,0:T(8,128)(2,1)S(1)} %get-tuple-element.58, bf16[2048,640]{1,0:T(8,128)(2,1)S(1)} %copy-done.66), kind=kOutput, calls=%fused_computation.22 | convolution fusion | flops 2734686208 | bytes 29097984 | tf_op jit(solution)/shard_map/nd,fd->nf/dot_general | solution.py:180
  170.5 7.1 %fusion.49 = f32[2,1024,256]{2,1,0:T(8,128)S(1)} fusion(bf16[2,512,4,256]{3,2,1,0:T(4,128)(2,1)S(1)} %reshape.295, f32[2,4,512,1024]{2,3,1,0:T(8,128)} %get-tuple-element.75, f32[2,4,512]{2,1,0:T(4,128)S(1)} %bitcast.156), kind=kOutput, calls=%fused_computation.111 | convolution fusion | flops 2155872256 | bytes 20987904 | tf_op jit(solution)/shard_map/shqk,sqhd->skd/dot_general | solution.py:211
  179.7 11.3 %fusion = (f32[2,4,512]{2,1,0:T(4,128)S(1)}, f32[2,1024,512,4]{2,1,3,0:T(8,128)}) fusion(f32[2,4,512,1024]{2,3,1,0:T(8,128)} %get-tuple-element.75, f32[2,4,512]{2,1,0:T(4,128)S(1)} %bitcast.157, bf16[2,512,4,256]{3,2,1,0:T(4,128)(2,1)S(1)} %reshape.295, bf16[2,512,256]{2,1,0:T(8,128)(2,1)S(1)} %slice.130, bf16[2,512,256]{2,1,0:T(8,128)(2,1)} %collective-permute-done), kind=kOutput, calls=%fused_computation.2 | convolution fusion | flops 2162159616 | bytes 36732928 | tf_op jit(solution)/shard_map/sqhd,skd->shqk/dot_general | solution.py:217
  191.1 12.1 %fusion.2 = bf16[2,4,512,1024]{2,3,1,0:T(8,128)(2,1)S(1)} fusion(f32[2,1024,512,4]{2,1,3,0:T(8,128)} %get-tuple-element.84, f32[2,4,512,1024]{2,3,1,0:T(8,128)} %get-tuple-element.75, f32[2,4,512]{2,1,0:T(4,128)S(1)} %get-tuple-element.83, f32[2,4,512]{2,1,0:T(4,128)S(1)} %bitcast.158), kind=kLoop, calls=%fused_computation.4 | loop fusion | flops 16777216 | bytes 41975808 | tf_op jit(solution)/shard_map/convert_element_type | solution.py:221
  205.6 4.8 multiply_bitcast_fusion
  216.4 11.4 %collective-permute-done.4 = bf16[2,512,256]{2,1,0:T(8,128)(2,1)S(1)} collective-permute-done((bf16[2,512,256]{2,1,0:T(8,128)(2,1)S(1)}, bf16[2,512,256]{2,1,0:T(8,128)(2,1)S(1)}, u32[]{:S(2)}, u32[]{:S(2)}) %collective-permute-start.4) | collective-permute-done | bytes 524320 | tf_op jit(solution)/shard_map/ppermute | solution.py:29
  242.5 7.6 %convolution_convert_fusion = bf16[2048,640]{1,0:T(8,128)(2,1)} fusion(bf16[1024,2048]{1,0:T(8,128)(2,1)} %get-tuple-element.78, bf16[1024,640]{1,0:T(8,128)(2,1)} %copy-done.26), kind=kOutput, calls=%fused_computation.49 | convolution fusion | flops 2685665280 | bytes 8126464 | tf_op jit(solution)/shard_map/nf,nd->fd/dot_general | solution.py:179
  251.5 5.4 fusion.22
  264.9 7.2 %fusion.35 = (bf16[640]{0:T(1024)(128)(2,1)S(1)}, f32[1024]{0:T(1024)S(1)}, f32[1024,640]{1,0:T(8,128)}) fusion(bf16[2,512,640]{2,1,0:T(8,128)(2,1)} %param.19, f32[1024]{0:T(1024)S(1)} %rsqrt.75, f32[640]{0:T(1024)S(1)} %copy-done.54, bf16[1024,1536]{1,0:T(8,128)(2,1)} %bitcast.150, bf16[640,1536]{1,0:T(8,128)(2,1)} %all-gather.6.cloned.1.call-done), kind=kOutput, calls=%fused_computation.76 | convolution fusion | flops 2017851776 | bytes 9056000 | tf_op jit(solution)/shard_map/nk,dk->nd/dot_general | solution.py:245
  273.3 5.7 all-reduce.7
  284.5 27.7 %reduce-scatter.11.cloned.1.call-done = bf16[512,640]{1,0:T(8,128)(2,1)} async-done(((bf16[2048,640]{1,0:T(8,128)(2,1)}), bf16[512,640]{1,0:T(8,128)(2,1)}) %reduce-scatter.11.cloned.1.call-update) | async-done | bytes 655376 | tf_op jit(solution)/shard_map/reduce_scatter | solution.py:273
  312.2 54.1 %reduce-scatter.9.cloned.1.call-done = bf16[2,640,512]{2,1,0:T(8,128)(2,1)} async-done(((bf16[2,640,2048]{2,1,0:T(8,128)(2,1)}), bf16[2,640,512]{2,1,0:T(8,128)(2,1)}) %reduce-scatter.9.cloned.1.call-update) | async-done | bytes 1310736 | tf_op jit(solution)/shard_map/reduce_scatter | solution.py:270
  366.3 222.0 %all-reduce.10 = (f32[640,384]{1,0:T(8,128)}, f32[256,640]{1,0:T(8,128)S(1)}, f32[2,640,512]{2,1,0:T(8,128)}, f32[512,640]{1,0:T(8,128)S(1)}, f32[768]{0:T(1024)S(1)}) all-reduce(bf16[640,384]{1,0:T(8,128)(2,1)S(1)} %copy.122, bf16[256,640]{1,0:T(8,128)(2,1)} %reduce-scatter.7.cloned.1.call-done, ...), channel_id=1, replica_groups=mesh['seq'=8,'shard'=4] {'seq'}, use_global_device_ids=true, to_apply=%region_16.17 | all-reduce | flops 1393408 | bytes 8361984 | tf_op jit(solution)/shard_map/psum | solution.py:285
  600.3 4.7 multiply_subtract_fusion
  (269 shorter events, 132.9 us)
Async XLA Ops:
  7.2 27.6 %all-gather.6.cloned.1.call-start = ((), (), s32[]{:S(2)}) async-start(), calls=%async_computation.4 | async-start | bytes 2457600 | tf_op jit(solution)/shard_map/all_gather | solution.py:119
  9.5 92.1 %all-gather.8.cloned.1.call-start = ((), (), s32[]{:S(2)}) async-start(), calls=%async_computation.5 | async-start | bytes 1638400 | tf_op jit(solution)/shard_map/all_gather | solution.py:120
  11.4 97.0 %all-gather.10.cloned.1.call-start = ((), (), s32[]{:S(2)}) async-start(), calls=%async_computation.6 | async-start | bytes 6553600 | tf_op jit(solution)/shard_map/all_gather | solution.py:121
  12.7 112.6 %all-gather.12.cloned.1.call-start = ((), (), s32[]{:S(2)}) async-start(), calls=%async_computation.7 | async-start | bytes 3276800 | tf_op jit(solution)/shard_map/all_gather | solution.py:122
  12.8 14.6 %collective-permute-start.1 = (s32[2,512]{1,0:T(2,128)S(1)}, s32[2,512]{1,0:T(2,128)S(1)}, u32[]{:S(2)}, u32[]{:S(2)}) collective-permute-start(s32[2,512]{1,0:T(2,128)S(1)} %copy-done.52), channel_id=1, source_target_pairs={{0,4},{4,8},{8,12},{12,16},{16,20},{20,24},{24,28},{1,5},{5,9},{9,... | collective-permute-start | bytes 12296 | tf_op jit(solution)/shard_map/ppermute | solution.py:29
  20.1 263.0 %reduce-scatter.7.cloned.1.call-start = ((), (), s32[]{:S(2)}) async-start(), calls=%async_computation.8 | async-start | bytes 1638400 | tf_op jit(solution)/shard_map/reduce_scatter | solution.py:267
  25.4 21.7 %copy-start.48 = (f32[256]{0:T(256)}, f32[256]{0:T(256)S(1)}, u32[]{:S(2)}) copy-start(f32[256]{0:T(256)S(1)} %get-tuple-element.68) | copy-start | bytes 3076
  25.4 37.9 %copy-start.50 = (f32[256]{0:T(256)}, f32[256]{0:T(256)S(1)}, u32[]{:S(2)}) copy-start(f32[256]{0:T(256)S(1)} %get-tuple-element.69) | copy-start | bytes 3076
  27.4 20.0 %copy-start.63 = (f32[128]{0:T(128)}, f32[128]{0:T(128)S(1)}, u32[]{:S(2)}) copy-start(f32[128]{0:T(128)S(1)} %negate_power_fusion) | copy-start | bytes 1540
  27.4 20.0 %copy-start.44 = (f32[2,512]{1,0:T(2,128)}, f32[2,512]{1,0:T(2,128)S(1)}, u32[]{:S(2)}) copy-start(f32[2,512]{1,0:T(2,128)S(1)} %convert_element_type.124) | copy-start | bytes 12292
  43.0 42.9 %collective-permute-start = (bf16[2,512,256]{2,1,0:T(8,128)(2,1)S(1)}, bf16[2,512,256]{2,1,0:T(8,128)(2,1)}, u32[]{:S(2)}, u32[]{:S(2)}) collective-permute-start(bf16[2,512,256]{2,1,0:T(8,128)(2,1)S(1)} %slice.130), channel_id=1, source_target_pairs={{0,4},{4,8},{8,12},{12,16},{16,20},{20,24},{24,28},{1,5},{5,9},{9,... | collective-permute-start | bytes 1572872 | tf_op jit(solution)/shard_map/ppermute | solution.py:29
  49.5 17.0 %copy-start.13 = (f32[2,512,128]{2,1,0:T(8,128)}, f32[2,512,128]{2,1,0:T(8,128)S(1)}, u32[]{:S(2)}) copy-start(f32[2,512,128]{2,1,0:T(8,128)S(1)} %get-tuple-element.70) | copy-start | bytes 1572868
  49.5 17.0 %copy-start.15 = (f32[2,512,128]{2,1,0:T(8,128)}, f32[2,512,128]{2,1,0:T(8,128)S(1)}, u32[]{:S(2)}) copy-start(f32[2,512,128]{2,1,0:T(8,128)S(1)} %get-tuple-element.71) | copy-start | bytes 1572868
  49.5 19.7 %copy-start.34 = (bf16[2,512,128]{2,1,0:T(8,128)(2,1)}, bf16[2,512,128]{2,1,0:T(8,128)(2,1)S(1)}, u32[]{:S(2)}) copy-start(bf16[2,512,128]{2,1,0:T(8,128)(2,1)S(1)} %get-tuple-element.63) | copy-start | bytes 786436
  50.5 18.7 %collective-permute-start.2 = (bf16[2,512,256]{2,1,0:T(8,128)(2,1)}, bf16[2,512,256]{2,1,0:T(8,128)(2,1)}, u32[]{:S(2)}, u32[]{:S(2)}) collective-permute-start(bf16[2,512,256]{2,1,0:T(8,128)(2,1)} %pad_maximum_fusion.4), channel_id=1, source_target_pairs={{0,4},{4,8},{8,12},{12,16},{16,20},{20,24},{24,28},{1,5},{5,9},{9,... | collective-permute-start | bytes 1572872 | tf_op jit(solution)/shard_map/ppermute | solution.py:29
  170.4 112.7 %reduce-scatter.13.cloned.1.call-start = ((), (), s32[]{:S(2)}) async-start(), calls=%async_computation.11 | async-start | bytes 2457600
  178.4 54.9 %collective-permute-start.3 = (bf16[2,512,256]{2,1,0:T(8,128)(2,1)}, bf16[2,512,256]{2,1,0:T(8,128)(2,1)S(1)}, u32[]{:S(2)}, u32[]{:S(2)}) collective-permute-start(bf16[2,512,256]{2,1,0:T(8,128)(2,1)} %slice.129), channel_id=1, source_target_pairs={{4,0},{8,4},{12,8},{16,12},{20,16},{24,20},{28,24},{5,1},{9,5},{13... | collective-permute-start | bytes 1572872 | tf_op jit(solution)/shard_map/ppermute | solution.py:29
  211.0 16.7 %collective-permute-start.4 = (bf16[2,512,256]{2,1,0:T(8,128)(2,1)S(1)}, bf16[2,512,256]{2,1,0:T(8,128)(2,1)S(1)}, u32[]{:S(2)}, u32[]{:S(2)}) collective-permute-start(bf16[2,512,256]{2,1,0:T(8,128)(2,1)S(1)} %slice.128), channel_id=1, source_target_pairs={{4,0},{8,4},{12,8},{16,12},{20,16},{24,20},{28,24},{5,1},{9,5},{13... | collective-permute-start | bytes 1572872 | tf_op jit(solution)/shard_map/ppermute | solution.py:29
  242.5 69.7 %reduce-scatter.11.cloned.1.call-start = ((), (), s32[]{:S(2)}) async-start(), calls=%async_computation.10 | async-start | bytes 3276800 | tf_op jit(solution)/shard_map/reduce_scatter | solution.py:273
  250.1 116.2 %reduce-scatter.9.cloned.1.call-start = ((), (), s32[]{:S(2)}) async-start(), calls=%async_computation.9 | async-start | bytes 6553600 | tf_op jit(solution)/shard_map/reduce_scatter | solution.py:270
  283.0 305.3 %copy-start.56 = (f32[768]{0:T(1024)S(1)}, f32[768]{0:T(1024)}, u32[]{:S(2)}) copy-start(f32[768]{0:T(1024)} %param.27) | copy-start | bytes 9220
  283.0 305.3 %copy-start.58 = (f32[768]{0:T(1024)S(1)}, f32[768]{0:T(1024)}, u32[]{:S(2)}) copy-start(f32[768]{0:T(1024)} %param.36) | copy-start | bytes 9220
  283.0 305.3 %copy-start.59 = (f32[768]{0:T(1024)S(1)}, f32[768]{0:T(1024)}, u32[]{:S(2)}) copy-start(f32[768]{0:T(1024)} %param.37) | copy-start | bytes 9220
  283.0 306.0 %copy-start.17 = (f32[640,384]{1,0:T(8,128)S(1)}, f32[640,384]{1,0:T(8,128)}, u32[]{:S(2)}) copy-start(f32[640,384]{1,0:T(8,128)} %param.23) | copy-start | bytes 2949124
  (64 other events, 380.0 us)
Sparse Core Ops, SparseCore 0:
  10.2 24.5 all-gather.5
  36.9 18.1 all-gather.7
  57.3 40.4 all-gather.9
  99.7 25.5 all-gather.11
  170.5 27.2 reduce-scatter.6
  242.6 31.7 reduce-scatter.12
  277.5 34.6 reduce-scatter.10
  314.9 51.3 reduce-scatter.8
where the time goes:
time: 618 us; the launch traced here: 612 us
  blocking collectives  233 us (38%)
  matrix products  126 us (20%)
  waiting for transfers between devices  101 us (16%)
  other arithmetic  80.2 us (13%)
  local copies, waits for them, and re-layouts  38.9 us (6%)
  between operations  16.5 us (3%)
  starting transfers between devices  16 us (3%)
    psum x1, blocking collectives, on_device(): lax.psum((shard_grads[0], shard_grads[1], shard_grads[2], shard_grads[3],...  222 us
    reduce_scatter x1, waiting for transfers between devices, on_device(): lax.psum_scatter(grad_ffin.astype(jnp.bfloat16), 'shard', scatter_dimensi...  54.1 us
    reduce_scatter x1, waiting for transfers between devices, on_device(): lax.psum_scatter(grad_ffout.astype(jnp.bfloat16), 'shard', scatter_dimens...  27.7 us
    unnamed x161, local copies, waits for them, and re-layouts  21.8 us
    ppermute x5, starting transfers between devices, from_behind(): return lax.ppermute(block, axis, route)  15.4 us
    ppermute x5, waiting for transfers between devices, from_behind(): return lax.ppermute(block, axis, route)  13.5 us
    dot_general x1, matrix products, on_device(): jnp.einsum('nd,fd->nf', grad_ffn_low, w_ffout, preferred_element_type=jnp...  13.5 us
    sub x5, other arithmetic, adam_step(): weight - step_rate * (moment_hat / (jnp.sqrt(square_hat) + adam_eps) + de...  13.5 us
  transfers between devices with their start and end apart: 13, of which 6 were waited for; matrix products, arithmetic and copies ran while one was open for 28% of the time, Pallas kernels for 0%

commit v1 on v0

--- a/solution.py
+++ b/solution.py
@@ -27,6 +27,60 @@
     devices = range(lax.axis_size(axis))
     route = [(i - distance, i) for i in devices if i - distance in devices]
     return lax.ppermute(block, axis, route)
+
+
+def swap_bit(block, axis, bit):
+    return lax.ppermute(block, axis, [(i, i ^ (1 << bit)) for i in range(lax.axis_size(axis))])
+
+
+def my_bit(axis, bit):
+    return (lax.axis_index(axis) >> bit) & 1
+
+
+def halve(block, axis, bit, at):
+    mine = my_bit(axis, bit)
+    sent = lax.dynamic_index_in_dim(block, 1 - mine, at, keepdims=False)
+    kept = lax.dynamic_index_in_dim(block, mine, at, keepdims=False)
+    came = swap_bit(sent, axis, bit)
+    return (kept.astype(jnp.float32) + came.astype(jnp.float32)).astype(jnp.bfloat16)
+
+
+def bits_of(axis):
+    return lax.axis_size(axis).bit_length() - 1
+
+
+def reduce_steps(block):
+    for bit in range(bits_of("shard")):
+        block = halve(block.reshape((-1, 2) + block.shape[1:]), "shard", bit, 1)
+        block = yield block
+    block = block[0]
+    for bit in range(bits_of("seq")):
+        block = halve(block.reshape((2, -1) + block.shape[1:]), "seq", bit, 0)
+        block = yield block
+    for bit in reversed(range(bits_of("seq"))):
+        came = swap_bit(block, "seq", bit)
+        low = my_bit("seq", bit) == 0
+        block = jnp.concatenate([jnp.where(low, block, came), jnp.where(low, came, block)], axis=0)
+        block = yield block
+
+
+def advance(steps, block):
+    try:
+        return steps.send(block)
+    except StopIteration:
+        return block
+
+
+def finish(steps, block):
+    while True:
+        try:
+            block = steps.send(block)
+        except StopIteration:
+            return block
+
+
+def together(*values):
+    return lax.optimization_barrier(values)
 
 
 def rms_scale(values, scales):
@@ -176,7 +230,6 @@
     post_back = jax.vjp(rms_scale, branch_two, gain_post)[1]
     grad_branch_two, grad_gain_post = post_back(cotangent)
     grad_ffn_low = grad_branch_two.astype(jnp.bfloat16)
-    grad_ffout = jnp.einsum("nf,nd->fd", hidden, grad_ffn_low, preferred_element_type=jnp.float32)
     grad_hidden = jnp.einsum("nd,fd->nf", grad_ffn_low, w_ffout, preferred_element_type=jnp.float32)
     gelu_back = jax.vjp(
         lambda gate_in, up_in: jax.nn.gelu(gate_in, approximate=True) * up_in, gate_proj, upward
@@ -184,12 +237,22 @@
     grad_gate, grad_up = gelu_back(grad_hidden)
     grad_gate_low = grad_gate.astype(jnp.bfloat16)
     grad_up_low = grad_up.astype(jnp.bfloat16)
-    grad_ffin = jnp.stack(
+    shards = lax.axis_size("shard")
+    low_dot = partial(jnp.einsum, preferred_element_type=jnp.float32)
+    ffn_parts = jnp.concatenate(
         [
-            jnp.einsum("nd,nf->df", normed_two, grad_gate_low, preferred_element_type=jnp.float32),
-            jnp.einsum("nd,nf->df", normed_two, grad_up_low, preferred_element_type=jnp.float32),
-        ]
-    )
+            part.astype(jnp.bfloat16).reshape(model_width, shards, -1).swapaxes(0, 1)
+            for part in (
+                low_dot("nd,nf->df", normed_two, grad_gate_low),
+                low_dot("nd,nf->df", normed_two, grad_up_low),
+                low_dot("nd,nf->df", grad_ffn_low, hidden),
+            )
+        ],
+        axis=1,
+    )
+    grad_gate_low, grad_up_low, ffn_parts = together(grad_gate_low, grad_up_low, ffn_parts)
+    ffn_steps = reduce_steps(ffn_parts)
+    ffn_sum = next(ffn_steps)
     grad_normed_two = jnp.einsum(
         "nf,df->nd", grad_gate_low, w_ffin[0], preferred_element_type=jnp.float32
     ) + jnp.einsum("nf,df->nd", grad_up_low, w_ffin[1], preferred_element_type=jnp.float32)
@@ -199,13 +262,12 @@
     attn_back = jax.vjp(rms_scale, branch, gain_attn)[1]
     grad_branch, grad_gain_attn = attn_back(grad_middle)
     grad_attn_low = grad_branch.astype(jnp.bfloat16)
-    grad_out = jnp.einsum(
-        "nk,nd->kd", attended_low, grad_attn_low, preferred_element_type=jnp.float32
-    )
     grad_attended = jnp.einsum(
         "nd,kd->nk", grad_attn_low, w_out, preferred_element_type=jnp.float32
     )
     grad_attended = grad_attended.astype(jnp.bfloat16).reshape(seqs_here, span_rows, QH, HEAD)
+    grad_attended, ffn_sum = together(grad_attended, ffn_sum)
+    ffn_sum = advance(ffn_steps, ffn_sum)
     scores_back = score_block(queries, all_keys, allowed)
     probs_back = jnp.exp(scores_back - log_total)
     grad_values = jnp.einsum(
@@ -219,6 +281,8 @@
     )
     inner_sum = jnp.sum(probs_back * grad_probs, axis=-1, keepdims=True)
     grad_scores = (probs_back * (grad_probs - inner_sum)).astype(jnp.bfloat16)
+    grad_scores, ffn_sum = together(grad_scores, ffn_sum)
+    ffn_sum = advance(ffn_steps, ffn_sum)
     grad_queries = jnp.einsum(
         "shqk,skd->sqhd", grad_scores, all_keys, preferred_element_type=jnp.float32
     ) * HEAD ** (-0.5)
@@ -241,7 +305,22 @@
         (grad_queries, grad_key_own, grad_value_own)
     )
     grad_project_low = grad_project.reshape(row_count, -1).astype(jnp.bfloat16)
-    grad_qkv = jnp.einsum("nd,nk->dk", normed, grad_project_low, preferred_element_type=jnp.float32)
+    grad_project_low, ffn_sum = together(grad_project_low, ffn_sum)
+    ffn_sum = advance(ffn_steps, ffn_sum)
+    attn_parts = jnp.concatenate(
+        [
+            part.astype(jnp.bfloat16).reshape(model_width, shards, -1).swapaxes(0, 1)
+            for part in (
+                low_dot("nd,nk->dk", normed, grad_project_low),
+                low_dot("nd,nk->dk", grad_attn_low, attended_low),
+            )
+        ],
+        axis=2,
+    )
+    grad_project_low, attn_parts = together(grad_project_low, attn_parts)
+    attn_steps = reduce_steps(attn_parts)
+    attn_total = finish(attn_steps, next(attn_steps))
+    ffn_total = finish(ffn_steps, ffn_sum)
     grad_normed = jnp.einsum(
         "nk,dk->nd", grad_project_low, w_qkv, preferred_element_type=jnp.float32
     )
@@ -260,30 +339,24 @@
             grad_gain_key,
         ]
     )
-    shard_grads = (
-        lax.psum_scatter(
-            grad_qkv.astype(jnp.bfloat16), "shard", scatter_dimension=1, tiled=True
-        ).astype(jnp.float32),
-        lax.psum_scatter(
-            grad_out.astype(jnp.bfloat16), "shard", scatter_dimension=0, tiled=True
-        ).astype(jnp.float32),
-        lax.psum_scatter(
-            grad_ffin.astype(jnp.bfloat16), "shard", scatter_dimension=2, tiled=True
-        ).astype(jnp.float32),
-        lax.psum_scatter(
-            grad_ffout.astype(jnp.bfloat16), "shard", scatter_dimension=0, tiled=True
-        ).astype(jnp.float32),
-        lax.psum_scatter(
-            grad_gains.astype(jnp.bfloat16), "shard", scatter_dimension=0, tiled=True
-        ).astype(jnp.float32),
-    )
     masters = (qkv_weight, out_weight, ff_in_weight, ff_out_weight, norm_gains)
     moments = (qkv_moment, out_moment, ff_in_moment, ff_out_moment, gains_moment)
     squares = (qkv_square, out_square, ff_in_square, ff_out_square, gains_square)
     step_rates = (rate_matrix, rate_matrix, rate_matrix, rate_matrix, rate_gain)
     decays = (decay_matrix, decay_matrix, decay_matrix, decay_matrix, 0.0)
-    totals = lax.psum(
-        (shard_grads[0], shard_grads[1], shard_grads[2], shard_grads[3], shard_grads[4]), "seq"
+    gains_here = norm_gains.shape[0]
+    gains_total = lax.dynamic_slice_in_dim(
+        lax.psum(grad_gains, ("shard", "seq")), lax.axis_index("shard") * gains_here, gains_here
+    )
+    qkv_here = qkv_weight.shape[1]
+    attn_total, ffn_total = together(attn_total, ffn_total)
+    down_total, out_total = together(ffn_total[2 * model_width :].T, attn_total[:, qkv_here:].T)
+    totals = (
+        attn_total[:, :qkv_here].astype(jnp.float32),
+        out_total.astype(jnp.float32),
+        ffn_total[: 2 * model_width].reshape(ff_in_weight.shape).astype(jnp.float32),
+        down_total.astype(jnp.float32),
+        gains_total,
     )
     results = [
         adam_step(

time: 618 us -> 495 us (0.80)
  blocking collectives: 233 us -> 56.8 us
  local copies, waits for them, and re-layouts: 38.9 us -> 72.4 us
  starting transfers between devices: 16 us -> 38.6 us
  other arithmetic: 80.2 us -> 102 us
  waiting for transfers between devices: 101 us -> 88.6 us
  matrix products: 126 us -> 114 us
    psum x1, blocking collectives: 222 us -> 51.6 us  [on_device(): lax.psum(grad_gains, ('shard', 'seq'))]
    reduce_scatter x3 -> x0, waiting for transfers between devices: 81.9 us -> none  [the longest x1 54.1 us: on_device(): lax.psum_scatter(grad_ffin.astype(jnp.bfloat16), 'shard', scatter_dimensi...]
    ppermute x0 -> x16, waiting for transfers between devices: none -> 63.6 us  [swap_bit(): lax.ppermute(block, axis, [(i, i ^ 1 << bit) for i in range(lax.axis_size...]
    ppermute x0 -> x16, starting transfers between devices: none -> 23.8 us  [swap_bit(): lax.ppermute(block, axis, [(i, i ^ 1 << bit) for i in range(lax.axis_size...]
    unnamed x161 -> x194, local copies, waits for them, and re-layouts: 21.8 us -> 44.8 us
    sub x0 -> x1, other arithmetic: none -> 22.9 us  [on_device(): grad_scores = (probs_back * (grad_probs - inner_sum)).astype(jnp.bfloat16)]
    dot_general x5, matrix products: 22.7 us -> 15.7 us  [the longest x1 3.58 us: on_device(): low_dot('nd,nf->df', grad_ffn_low, hidden)]
    squeeze x0 -> x10, local copies, waits for them, and re-layouts: none -> 6.23 us  [halve(): sent = lax.dynamic_index_in_dim(block, 1 - mine, at, keepdims=False)]
  transfers between devices with their start and end apart: 13 -> 25, of which waited for: 6 -> 14; matrix products, arithmetic and copies ran while one was open for 28% -> 37% of each run, Pallas kernels for 0% -> 0%
where the time goes in v1:
time: 495 us; the launch traced here: 487 us
  matrix products  114 us (23%)
  other arithmetic  102 us (21%)
  waiting for transfers between devices  88.6 us (18%)
  local copies, waits for them, and re-layouts  72.4 us (15%)
  blocking collectives  56.8 us (11%)
  starting transfers between devices  38.6 us (8%)
  between operations  15.7 us (3%)
    ppermute x16, waiting for transfers between devices, swap_bit(): lax.ppermute(block, axis, [(i, i ^ 1 << bit) for i in range(lax.axis_size...  63.6 us
    psum x1, blocking collectives, on_device(): lax.psum(grad_gains, ('shard', 'seq'))  51.6 us
    unnamed x194, local copies, waits for them, and re-layouts  44.8 us
    ppermute x16, starting transfers between devices, swap_bit(): lax.ppermute(block, axis, [(i, i ^ 1 << bit) for i in range(lax.axis_size...  23.8 us
    sub x1, other arithmetic, on_device(): grad_scores = (probs_back * (grad_probs - inner_sum)).astype(jnp.bfloat16)  22.9 us
    ppermute x5, waiting for transfers between devices, from_behind(): return lax.ppermute(block, axis, route)  17.9 us
    sub x5, other arithmetic, adam_step(): weight - step_rate * (moment_hat / (jnp.sqrt(square_hat) + adam_eps) + de...  17.4 us
    ppermute x5, starting transfers between devices, from_behind(): return lax.ppermute(block, axis, route)  14.6 us
  transfers between devices with their start and end apart: 25, of which 14 were waited for; matrix products, arithmetic and copies ran while one was open for 37% of the time, Pallas kernels for 0%

profile of v1, /device:TPU:0, one launch (start us, length us, event | category | flops | bytes accessed | tf_op | source)
XLA Modules:
  0.0 487.4 jit_solution(12112094850103926305)
XLA Ops:
  12.8 5.0 %collective-permute-start.1 = (s32[2,512]{1,0:T(2,128)S(1)}, s32[2,512]{1,0:T(2,128)S(1)}, u32[]{:S(2)}, u32[]{:S(2)}) collective-permute-start(s32[2,512]{1,0:T(2,128)S(1)} %copy-done.67), channel_id=1, source_target_pairs={{0,4},{4,8},{8,12},{12,16},{16,20},{20,24},{24,28},{1,5},{5,9},{9,... | collective-permute-start | bytes 12296 | tf_op jit(solution)/shard_map/ppermute | solution.py:29
  20.1 5.2 %all-gather = bf16[4,1,768]{2,1,0:T(2,128)(2,1)S(1)} all-gather(bf16[1,1,768]{2,1,0:T(2,128)(2,1)S(1)} %reshape.375), channel_id=1, replica_groups=mesh['seq'=8,'shard'=4] {'shard'}, dimensions={0}, use_global_device_ids=true | all-gather | bytes 7680 | tf_op jit(solution)/shard_map/all_gather | solution.py:177
  27.8 7.0 %all-gather.6.cloned.1.call-done = bf16[640,1536]{1,0:T(8,128)(2,1)} async-done(((bf16[640,384]{1,0:T(8,128)(2,1)}), bf16[640,1536]{1,0:T(8,128)(2,1)}) %all-gather.6.cloned.1.call-update) | async-done | bytes 1966096 | tf_op jit(solution)/shard_map/all_gather | solution.py:173
  43.0 5.9 %reshape.346 = f32[2,512,4,256]{3,2,1,0:T(4,128)} reshape(f32[2,512,1024]{2,1,0:T(8,128)} %slice.105) | data formatting | bytes 8388608 | tf_op jit(solution)/shard_map/reshape | solution.py:121
  64.7 7.4 %collective-permute-done.2 = bf16[2,512,256]{2,1,0:T(8,128)(2,1)S(1)} collective-permute-done((bf16[2,512,256]{2,1,0:T(8,128)(2,1)S(1)}, bf16[2,512,256]{2,1,0:T(8,128)(2,1)S(1)}, u32[]{:S(2)}, u32[]{:S(2)}) %collective-permute-start.2) | collective-permute-done | bytes 524320 | tf_op jit(solution)/shard_map/ppermute | solution.py:29
  72.1 7.5 %fusion.113 = (f32[2,4,512]{2,1,0:T(4,128)S(1)}, f32[2,4,512,1024]{2,3,1,0:T(8,128)}) fusion(bf16[2,512,4,128]{3,1,2,0:T(8,128)(2,1)S(1)} %get-tuple-element.184, bf16[2,512,4,128]{3,1,2,0:T(8,128)(2,1)S(1)} %get-tuple-element.183, bf16[2,512,128]{2,1,0:T(8,128)(2,1)S(1)} %get-tuple-element.193, bf16[2,512,128]{2,1,0:T(8,128)(2,1)S(1)} %get-tuple-element.192, ...), kind=kOutput, calls=%fused_computation.259 | convolution fusion | flops 2167402496 | bytes 20987904 | tf_op jit(solution)/shard_map/sqhd,skd->shqk/dot_general | solution.py:132
  79.6 8.1 %fusion.3 = f32[2,4,512]{2,1,0:T(4,128)S(1)} fusion(f32[2,4,512,1024]{2,3,1,0:T(8,128)} %get-tuple-element.215, f32[2,4,512]{2,1,0:T(4,128)S(1)} %get-tuple-element.214), kind=kLoop, calls=%fused_computation.9 | loop fusion | flops 8384512 | bytes 16809984 | tf_op jit(solution)/shard_map/reduce_sum | solution.py:207
  88.5 10.3 %convert_bitcast_fusion = bf16[2,512,4,256]{1,3,2,0:T(8,128)(2,1)} fusion(f32[2,4,512,1024]{2,3,1,0:T(8,128)} %get-tuple-element.215, f32[2,4,512]{2,1,0:T(4,128)S(1)} %fusion.3, f32[2,4,512]{2,1,0:T(4,128)S(1)} %get-tuple-element.214, bf16[2,512,256]{2,1,0:T(8,128)(2,1)S(1)} %slice.150, bf16[2,512,256]{2,1,0:T(8,128)(2,1)S(1)} %collective-permute-done), kind=kOutput, calls=%fused_computation.109 | convolution fusion | flops 2163212288 | bytes 19955712 | tf_op jit(solution)/shard_map/shqk,skd->sqhd/dot_general | solution.py:210
  111.5 5.7 %fusion.41 = f32[1024,2048]{1,0:T(8,128)S(1)} fusion(bf16[1024,640]{1,0:T(8,128)(2,1)} %multiply_convert_fusion.2, bf16[2,640,2048]{2,1,0:T(8,128)(2,1)} %all-gather.10.cloned.1.call-done), kind=kOutput, calls=%fused_computation.102 | convolution fusion | flops 2684354560 | bytes 12320768 | tf_op jit(solution)/shard_map/dot_general | solution.py:220
  120.6 7.6 %multiply_convert_fusion.1 = (bf16[1024,2048]{1,0:T(8,128)(2,1)}, f32[1024,2048]{1,0:T(8,128)}) fusion(f32[1024,2048]{1,0:T(8,128)S(1)} %fusion.41, bf16[1024,640]{1,0:T(8,128)(2,1)S(1)} %copy-done.33, bf16[2,640,2048]{2,1,0:T(8,128)(2,1)S(1)} %copy-done.76), kind=kOutput, calls=%fused_computation.23 | convolution fusion | flops 2705326080 | bytes 24903680 | tf_op jit(solution)/shard_map/dot_general | solution.py:221
  128.2 6.2 %multiply_reduce_fusion.6 = (f32[1024]{0:T(1024)S(1)}, f32[1024,640]{1,0:T(8,128)S(1)}) fusion(bf16[1024,2048]{1,0:T(8,128)(2,1)} %get-tuple-element.218, bf16[2048,640]{1,0:T(8,128)(2,1)} %all-gather.12.cloned.1.call-done), kind=kOutput, calls=%fused_computation.97 | convolution fusion | flops 2685664256 | bytes 9441280 | tf_op jit(solution)/shard_map/dot_general | solution.py:223
  142.3 12.8 %multiply_convert_fusion = (bf16[1024,2048]{1,0:T(8,128)(2,1)S(1)}, bf16[1024,2048]{1,0:T(8,128)(2,1)}) fusion(f32[1024,2048]{1,0:T(8,128)} %copy-done.81, f32[1024,2048]{1,0:T(8,128)} %get-tuple-element.219, bf16[1024,640]{1,0:T(8,128)(2,1)S(1)} %get-tuple-element.185, bf16[2048,640]{1,0:T(8,128)(2,1)S(1)} %copy-done.77), kind=kOutput, calls=%fused_computation.22 | convolution fusion | flops 2734686208 | bytes 29097984 | tf_op jit(solution)/shard_map/nd,fd->nf/dot_general | solution.py:233
  199.1 9.5 %fusion.54 = f32[2,1024,256]{2,1,0:T(8,128)} fusion(bf16[2,512,4,256]{3,2,1,0:T(4,128)(2,1)S(1)} %reshape.353, f32[2,4,512,1024]{2,3,1,0:T(8,128)} %get-tuple-element.215, f32[2,4,512]{2,1,0:T(4,128)S(1)} %bitcast.260), kind=kOutput, calls=%fused_computation.131 | convolution fusion | flops 2155872256 | bytes 20987904 | tf_op jit(solution)/shard_map/shqk,sqhd->skd/dot_general | solution.py:273
  212.0 8.2 %fusion.51 = f32[2,1024,512,4]{2,1,3,0:T(8,128)} fusion(bf16[2,512,4,256]{3,2,1,0:T(4,128)(2,1)S(1)} %reshape.353, bf16[2,512,256]{2,1,0:T(8,128)(2,1)S(1)} %copy-done.31, bf16[2,512,256]{2,1,0:T(8,128)(2,1)S(1)} %copy-done.46), kind=kOutput, calls=%fused_computation.125 | convolution fusion | flops 2149580800 | bytes 19922944 | tf_op jit(solution)/shard_map/sqhd,skd->shqk/dot_general | solution.py:279
  220.2 22.9 %fusion.2 = bf16[2,4,512,1024]{2,3,1,0:T(8,128)(2,1)S(1)} fusion(f32[2,1024,512,4]{2,1,3,0:T(8,128)} %fusion.51, f32[2,4,512,1024]{2,3,1,0:T(8,128)} %get-tuple-element.215, f32[2,4,512]{2,1,0:T(4,128)S(1)} %bitcast.261), kind=kOutput, calls=%fused_computation.4 | output fusion | flops 25170944 | bytes 41959424 | tf_op jit(solution)/shard_map/sub | solution.py:283
  263.4 10.5 %collective-permute-done.6 = bf16[2,512,256]{2,1,0:T(8,128)(2,1)S(1)} collective-permute-done((bf16[2,512,256]{2,1,0:T(8,128)(2,1)S(1)}, bf16[2,512,256]{2,1,0:T(8,128)(2,1)S(1)}, u32[]{:S(2)}, u32[]{:S(2)}) %collective-permute-start.6) | collective-permute-done | bytes 524320 | tf_op jit(solution)/shard_map/ppermute | solution.py:29
  280.2 13.7 %collective-permute-done.7 = bf16[960,512]{1,0:T(8,128)(2,1)S(1)} collective-permute-done((bf16[960,512]{1,0:T(8,128)(2,1)S(1)}, bf16[960,512]{1,0:T(8,128)(2,1)S(1)}, u32[]{:S(2)}, u32[]{:S(2)}) %collective-permute-start.7) | collective-permute-done | bytes 983072 | tf_op jit(solution)/shard_map/ppermute | solution.py:33
  319.2 5.7 %fusion.35 = (f32[640]{0:T(1024)S(1)}, f32[1024]{0:T(1024)S(1)}, f32[1024,640]{1,0:T(8,128)S(1)}) fusion(bf16[2,512,640]{2,1,0:T(8,128)(2,1)} %param.19, f32[1024]{0:T(1024)S(1)} %copy-done.54, f32[640]{0:T(1024)S(1)} %copy-done.56, bf16[1024,1536]{1,0:T(8,128)(2,1)} %bitcast.244, bf16[640,1536]{1,0:T(8,128)(2,1)} %all-gather.6.cloned.1.call-done), kind=kOutput, calls=%fused_computation.86 | convolution fusion | flops 2017851776 | bytes 9057280 | tf_op jit(solution)/shard_map/nk,dk->nd/dot_general | solution.py:324
  334.0 11.3 %collective-permute-done.17 = bf16[240,512]{1,0:T(8,128)(2,1)S(1)} collective-permute-done((bf16[240,512]{1,0:T(8,128)(2,1)S(1)}, bf16[240,512]{1,0:T(8,128)(2,1)S(1)}, u32[]{:S(2)}, u32[]{:S(2)}) %collective-permute-start.17) | collective-permute-done | bytes 245792 | tf_op jit(solution)/shard_map/ppermute | solution.py:33
  352.0 6.6 %collective-permute-done.18 = bf16[240,512]{1,0:T(8,128)(2,1)S(1)} collective-permute-done((bf16[240,512]{1,0:T(8,128)(2,1)S(1)}, bf16[240,512]{1,0:T(8,128)(2,1)S(1)}, u32[]{:S(2)}, u32[]{:S(2)}) %collective-permute-start.18) | collective-permute-done | bytes 245792 | tf_op jit(solution)/shard_map/ppermute | solution.py:33
  362.1 10.2 %collective-permute-done.19 = bf16[480,512]{1,0:T(8,128)(2,1)S(1)} collective-permute-done((bf16[480,512]{1,0:T(8,128)(2,1)S(1)}, bf16[480,512]{1,0:T(8,128)(2,1)S(1)}, u32[]{:S(2)}, u32[]{:S(2)}) %collective-permute-start.19) | collective-permute-done | bytes 491552 | tf_op jit(solution)/shard_map/ppermute | solution.py:33
  382.1 51.6 %psum.7 = f32[3072]{0:T(1024)S(1)} all-reduce(f32[3072]{0:T(1024)S(1)} %constant_dynamic-update-slice_fusion), channel_id=1, replica_groups=mesh['seq'=8,'shard'=4] {'shard','seq'}, use_global_device_ids=true, to_apply=%region_21.22 | all-reduce | flops 3072 | bytes 24576 | tf_op jit(solution)/shard_map/psum | solution.py:349
  442.6 6.9 %collective-permute-done.15 = bf16[320,640]{1,0:T(8,128)(2,1)S(1)} collective-permute-done((bf16[320,640]{1,0:T(8,128)(2,1)S(1)}, bf16[320,640]{1,0:T(8,128)(2,1)S(1)}, u32[]{:S(2)}, u32[]{:S(2)}) %collective-permute-start.15) | collective-permute-done | bytes 409632 | tf_op jit(solution)/shard_map/ppermute | solution.py:33
  473.4 7.3 %multiply_subtract_fusion = (f32[2,640,512]{2,1,0:T(8,128)}, f32[2,640,512]{2,1,0:T(8,128)}, f32[2,640,512]{2,1,0:T(8,128)}) fusion(f32[2,640,512]{2,1,0:T(8,128)S(1)} %copy-done.13, bf16[2,640,512]{2,1,0:T(8,128)(2,1)S(1)} %bitcast.236, f32[2,640,512]{2,1,0:T(8,128)} %param.32, f32[2,640,512]{2,1,0:T(8,128)} %param.33), kind=kLoop, calls=%fused_computation.93 | loop fusion | flops 10485760 | bytes 17039360 | tf_op jit(solution)/shard_map/sub | solution.py:143
  (361 shorter events, 218.7 us)
Async XLA Ops:
  7.2 27.6 %all-gather.6.cloned.1.call-start = ((), (), s32[]{:S(2)}) async-start(), calls=%async_computation | async-start | bytes 2457600 | tf_op jit(solution)/shard_map/all_gather | solution.py:173
  9.5 94.5 %all-gather.8.cloned.1.call-start = ((), (), s32[]{:S(2)}) async-start(), calls=%async_computation.1 | async-start | bytes 1638400 | tf_op jit(solution)/shard_map/all_gather | solution.py:174
  11.4 100.1 %all-gather.10.cloned.1.call-start = ((), (), s32[]{:S(2)}) async-start(), calls=%async_computation.2 | async-start | bytes 6553600 | tf_op jit(solution)/shard_map/all_gather | solution.py:175
  12.7 115.5 %all-gather.12.cloned.1.call-start = ((), (), s32[]{:S(2)}) async-start(), calls=%async_computation.3 | async-start | bytes 3276800 | tf_op jit(solution)/shard_map/all_gather | solution.py:176
  12.8 14.1 %collective-permute-start.1 = (s32[2,512]{1,0:T(2,128)S(1)}, s32[2,512]{1,0:T(2,128)S(1)}, u32[]{:S(2)}, u32[]{:S(2)}) collective-permute-start(s32[2,512]{1,0:T(2,128)S(1)} %copy-done.67), channel_id=1, source_target_pairs={{0,4},{4,8},{8,12},{12,16},{16,20},{20,24},{24,28},{1,5},{5,9},{9,... | collective-permute-start | bytes 12296 | tf_op jit(solution)/shard_map/ppermute | solution.py:29
  56.4 15.6 %collective-permute-start.2 = (bf16[2,512,256]{2,1,0:T(8,128)(2,1)S(1)}, bf16[2,512,256]{2,1,0:T(8,128)(2,1)S(1)}, u32[]{:S(2)}, u32[]{:S(2)}) collective-permute-start(bf16[2,512,256]{2,1,0:T(8,128)(2,1)S(1)} %pad_maximum_fusion.8), channel_id=1, source_target_pairs={{0,4},{4,8},{8,12},{12,16},{16,20},{20,24},{24,28},{1,5},{5,9},{9,... | collective-permute-start | bytes 1572872 | tf_op jit(solution)/shard_map/ppermute | solution.py:29
  59.8 27.8 %collective-permute-start = (bf16[2,512,256]{2,1,0:T(8,128)(2,1)S(1)}, bf16[2,512,256]{2,1,0:T(8,128)(2,1)S(1)}, u32[]{:S(2)}, u32[]{:S(2)}) collective-permute-start(bf16[2,512,256]{2,1,0:T(8,128)(2,1)S(1)} %slice.150), channel_id=1, source_target_pairs={{0,4},{4,8},{8,12},{12,16},{16,20},{20,24},{24,28},{1,5},{5,9},{9,... | collective-permute-start | bytes 1572872 | tf_op jit(solution)/shard_map/ppermute | solution.py:29
  168.7 24.1 %collective-permute-start.3 = (bf16[2,1920,512]{2,1,0:T(8,128)(2,1)}, bf16[2,1920,512]{2,1,0:T(8,128)(2,1)}, u32[]{:S(2)}, u32[]{:S(2)}) collective-permute-start(bf16[2,1920,512]{2,1,0:T(8,128)(2,1)} %dynamic-slice_bitcast_fusion), channel_id=1, source_target_pairs={{0,1},{1,0},{2,3},{3,2},{4,5},{5,4},{6,7},{7,6},{8,9},{9,8},{10,11... | collective-permute-start | bytes 11796488 | tf_op jit(solution)/shard_map/ppermute | solution.py:33
  198.6 45.6 %collective-permute-start.5 = (bf16[1,1920,512]{2,1,0:T(8,128)(2,1)}, bf16[1,1920,512]{2,1,0:T(8,128)(2,1)}, u32[]{:S(2)}, u32[]{:S(2)}) collective-permute-start(bf16[1,1920,512]{2,1,0:T(8,128)(2,1)} %constant_dynamic-slice_fusion.1), channel_id=1, source_target_pairs={{0,2},{1,3},{2,0},{3,1},{4,6},{5,7},{6,4},{7,5},{8,10},{9,11},{10,... | collective-permute-start | bytes 5898248 | tf_op jit(solution)/shard_map/ppermute | solution.py:33
  210.7 32.4 %collective-permute-start.4 = (bf16[2,512,256]{2,1,0:T(8,128)(2,1)}, bf16[2,512,256]{2,1,0:T(8,128)(2,1)}, u32[]{:S(2)}, u32[]{:S(2)}) collective-permute-start(bf16[2,512,256]{2,1,0:T(8,128)(2,1)} %slice.149), channel_id=1, source_target_pairs={{4,0},{8,4},{12,8},{16,12},{20,16},{24,20},{28,24},{5,1},{9,5},{13... | collective-permute-start | bytes 1572872 | tf_op jit(solution)/shard_map/ppermute | solution.py:29
  256.1 17.8 %collective-permute-start.6 = (bf16[2,512,256]{2,1,0:T(8,128)(2,1)S(1)}, bf16[2,512,256]{2,1,0:T(8,128)(2,1)S(1)}, u32[]{:S(2)}, u32[]{:S(2)}) collective-permute-start(bf16[2,512,256]{2,1,0:T(8,128)(2,1)S(1)} %slice.148), channel_id=1, source_target_pairs={{4,0},{8,4},{12,8},{16,12},{20,16},{24,20},{28,24},{5,1},{9,5},{13... | collective-permute-start | bytes 1572872 | tf_op jit(solution)/shard_map/ppermute | solution.py:29
  259.6 34.2 %collective-permute-start.7 = (bf16[960,512]{1,0:T(8,128)(2,1)S(1)}, bf16[960,512]{1,0:T(8,128)(2,1)S(1)}, u32[]{:S(2)}, u32[]{:S(2)}) collective-permute-start(bf16[960,512]{1,0:T(8,128)(2,1)S(1)} %dynamic-slice_bitcast_fusion.2), channel_id=1, source_target_pairs={{0,4},{4,0},{8,12},{12,8},{16,20},{20,16},{24,28},{28,24},{1,5},{5... | collective-permute-start | bytes 2949128 | tf_op jit(solution)/shard_map/ppermute | solution.py:33
  300.4 26.4 %collective-permute-start.8 = (bf16[2,640,640]{2,1,0:T(8,128)(2,1)}, bf16[2,640,640]{2,1,0:T(8,128)(2,1)}, u32[]{:S(2)}, u32[]{:S(2)}) collective-permute-start(bf16[2,640,640]{2,1,0:T(8,128)(2,1)} %dynamic-slice_bitcast_fusion.1), channel_id=1, source_target_pairs={{0,1},{1,0},{2,3},{3,2},{4,5},{5,4},{6,7},{7,6},{8,9},{9,8},{10,11... | collective-permute-start | bytes 4915208 | tf_op jit(solution)/shard_map/ppermute | solution.py:33
  316.3 14.8 %collective-permute-start.16 = (bf16[480,512]{1,0:T(8,128)(2,1)S(1)}, bf16[480,512]{1,0:T(8,128)(2,1)S(1)}, u32[]{:S(2)}, u32[]{:S(2)}) collective-permute-start(bf16[480,512]{1,0:T(8,128)(2,1)S(1)} %dynamic-slice_bitcast_fusion.3), channel_id=1, source_target_pairs={{0,8},{4,12},{8,0},{12,4},{16,24},{20,28},{24,16},{28,20},{1,9},{5... | collective-permute-start | bytes 1474568 | tf_op jit(solution)/shard_map/ppermute | solution.py:33
  328.7 20.4 %collective-permute-start.9 = (bf16[1,640,640]{2,1,0:T(8,128)(2,1)S(1)}, bf16[1,640,640]{2,1,0:T(8,128)(2,1)S(1)}, u32[]{:S(2)}, u32[]{:S(2)}) collective-permute-start(bf16[1,640,640]{2,1,0:T(8,128)(2,1)S(1)} %constant_dynamic-slice_fusion), channel_id=1, source_target_pairs={{0,2},{1,3},{2,0},{3,1},{4,6},{5,7},{6,4},{7,5},{8,10},{9,11},{10,... | collective-permute-start | bytes 2457608 | tf_op jit(solution)/shard_map/ppermute | solution.py:33
  331.3 14.0 %collective-permute-start.17 = (bf16[240,512]{1,0:T(8,128)(2,1)S(1)}, bf16[240,512]{1,0:T(8,128)(2,1)S(1)}, u32[]{:S(2)}, u32[]{:S(2)}) collective-permute-start(bf16[240,512]{1,0:T(8,128)(2,1)S(1)} %dynamic-slice_bitcast_fusion.5), channel_id=1, source_target_pairs={{0,16},{4,20},{8,24},{12,28},{16,0},{20,4},{24,8},{28,12},{1,17},{... | collective-permute-start | bytes 737288 | tf_op jit(solution)/shard_map/ppermute | solution.py:33
  345.4 13.2 %collective-permute-start.18 = (bf16[240,512]{1,0:T(8,128)(2,1)S(1)}, bf16[240,512]{1,0:T(8,128)(2,1)S(1)}, u32[]{:S(2)}, u32[]{:S(2)}) collective-permute-start(bf16[240,512]{1,0:T(8,128)(2,1)S(1)} %fusion.85), channel_id=1, source_target_pairs={{0,16},{4,20},{8,24},{12,28},{16,0},{20,4},{24,8},{28,12},{1,17},{... | collective-permute-start | bytes 737288 | tf_op jit(solution)/shard_map/ppermute | solution.py:33
  349.4 11.6 %collective-permute-start.10 = (bf16[320,640]{1,0:T(8,128)(2,1)S(1)}, bf16[320,640]{1,0:T(8,128)(2,1)S(1)}, u32[]{:S(2)}, u32[]{:S(2)}) collective-permute-start(bf16[320,640]{1,0:T(8,128)(2,1)S(1)} %dynamic-slice_bitcast_fusion.4), channel_id=1, source_target_pairs={{0,4},{4,0},{8,12},{12,8},{16,20},{20,16},{24,28},{28,24},{1,5},{5... | collective-permute-start | bytes 1228808 | tf_op jit(solution)/shard_map/ppermute | solution.py:33
  358.6 13.7 %collective-permute-start.19 = (bf16[480,512]{1,0:T(8,128)(2,1)S(1)}, bf16[480,512]{1,0:T(8,128)(2,1)S(1)}, u32[]{:S(2)}, u32[]{:S(2)}) collective-permute-start(bf16[480,512]{1,0:T(8,128)(2,1)S(1)} %pad_maximum_fusion.9), channel_id=1, source_target_pairs={{0,8},{4,12},{8,0},{12,4},{16,24},{20,28},{24,16},{28,20},{1,9},{5... | collective-permute-start | bytes 1474568 | tf_op jit(solution)/shard_map/ppermute | solution.py:33
  361.2 13.3 %collective-permute-start.11 = (bf16[160,640]{1,0:T(8,128)(2,1)S(1)}, bf16[160,640]{1,0:T(8,128)(2,1)S(1)}, u32[]{:S(2)}, u32[]{:S(2)}) collective-permute-start(bf16[160,640]{1,0:T(8,128)(2,1)S(1)} %dynamic-slice_bitcast_fusion.6), channel_id=1, source_target_pairs={{0,8},{4,12},{8,0},{12,4},{16,24},{20,28},{24,16},{28,20},{1,9},{5... | collective-permute-start | bytes 614408 | tf_op jit(solution)/shard_map/ppermute | solution.py:33
  374.6 6.7 %collective-permute-start.12 = (bf16[80,640]{1,0:T(8,128)(2,1)S(1)}, bf16[80,640]{1,0:T(8,128)(2,1)S(1)}, u32[]{:S(2)}, u32[]{:S(2)}) collective-permute-start(bf16[80,640]{1,0:T(8,128)(2,1)S(1)} %dynamic-slice_bitcast_fusion.7), channel_id=1, source_target_pairs={{0,16},{4,20},{8,24},{12,28},{16,0},{20,4},{24,8},{28,12},{1,17},{... | collective-permute-start | bytes 307208 | tf_op jit(solution)/shard_map/ppermute | solution.py:33
  376.5 65.6 %collective-permute-start.20 = (bf16[960,512]{1,0:T(8,128)(2,1)S(1)}, bf16[960,512]{1,0:T(8,128)(2,1)S(1)}, u32[]{:S(2)}, u32[]{:S(2)}) collective-permute-start(bf16[960,512]{1,0:T(8,128)(2,1)S(1)} %pad_maximum_fusion.6), channel_id=1, source_target_pairs={{0,4},{4,0},{8,12},{12,8},{16,20},{20,16},{24,28},{28,24},{1,5},{5... | collective-permute-start | bytes 2949128 | tf_op jit(solution)/shard_map/ppermute | solution.py:33
  381.3 52.3 %collective-permute-start.13 = (bf16[80,640]{1,0:T(8,128)(2,1)S(1)}, bf16[80,640]{1,0:T(8,128)(2,1)S(1)}, u32[]{:S(2)}, u32[]{:S(2)}) collective-permute-start(bf16[80,640]{1,0:T(8,128)(2,1)S(1)} %fusion.87), channel_id=1, source_target_pairs={{0,16},{4,20},{8,24},{12,28},{16,0},{20,4},{24,8},{28,12},{1,17},{... | collective-permute-start | bytes 307208 | tf_op jit(solution)/shard_map/ppermute | solution.py:33
  439.9 9.5 %collective-permute-start.15 = (bf16[320,640]{1,0:T(8,128)(2,1)S(1)}, bf16[320,640]{1,0:T(8,128)(2,1)S(1)}, u32[]{:S(2)}, u32[]{:S(2)}) collective-permute-start(bf16[320,640]{1,0:T(8,128)(2,1)S(1)} %pad_maximum_fusion.10), channel_id=1, source_target_pairs={{0,4},{4,0},{8,12},{12,8},{16,20},{20,16},{24,28},{28,24},{1,5},{5... | collective-permute-start | bytes 1228808 | tf_op jit(solution)/shard_map/ppermute | solution.py:33
  (89 other events, 1106.5 us)
Sparse Core Ops, SparseCore 0:
  10.2 24.5 all-gather.5
  36.9 18.1 all-gather.7
  57.3 40.4 all-gather.9
  99.7 25.5 all-gather.11

commit v2 on v1

--- a/solution.py
+++ b/solution.py
@@ -3,6 +3,8 @@
 import jax
 import jax.numpy as jnp
 from jax import lax
+from jax.experimental import pallas as pl
+from jax.experimental.pallas import tpu as pltpu
 from jax.sharding import PartitionSpec as P
 
 D = 640
@@ -126,6 +128,181 @@
     )
     key_rows = rotate(rms_scale(key_rows, gain_key), cos_table, sine_table)
     return (queries, key_rows, value_rows)
+
+
+f32 = jnp.float32
+bf16 = jnp.bfloat16
+row_block = 256
+vmem_most = 56 * 1024 * 1024
+
+
+def dot_nn(a, b):
+    return lax.dot_general(a, b, (((1,), (0,)), ((), ())), preferred_element_type=f32)
+
+
+def dot_nt(a, b):
+    return lax.dot_general(a, b, (((1,), (1,)), ((), ())), preferred_element_type=f32)
+
+
+def inverse_rms(v):
+    return lax.rsqrt(jnp.mean(v * v, axis=-1, keepdims=True) + eps_norm)
+
+
+def rms_back(v, r, gain, dy):
+    gdy = gain * dy
+    return r * gdy - v * (r * r * r) * jnp.mean(gdy * v, axis=-1, keepdims=True)
+
+
+def middle_kernel(
+    blocks, shards,
+    x_ref, o_ref, e_ref, w_out_ref, w_in_ref, w_down_ref, gains_ref,
+    mixed_ref, dx2_ref, do_ref, ffn_ref, out_ref, dgains_ref,
+    act, slope, h2_all, dm_all, db_all, o_all, hid_all, dg_all, du_all,
+):
+    step = pl.program_id(0)
+    ff = w_in_ref.shape[3]
+    model = x_ref.shape[1]
+    heads = out_ref.shape[2]
+
+    @pl.when(step < blocks)
+    def _():
+        rows = pl.ds(pl.multiple_of(step * row_block, row_block), row_block)
+        gain_attn, gain_pre, gain_post = gains_ref[0:1], gains_ref[1:2], gains_ref[2:3]
+        x = x_ref[...].astype(f32)
+        e = e_ref[...].astype(f32)
+        o = o_ref[...]
+        branch = dot_nn(o, w_out_ref[...])
+        r_branch = inverse_rms(branch)
+        x2 = x + branch * r_branch * gain_attn
+        r_x2 = inverse_rms(x2)
+        h2 = (x2 * r_x2 * gain_pre).astype(bf16)
+        m = jnp.zeros((row_block, model), f32)
+        for s in range(shards):
+            cols = slice(s * ff, (s + 1) * ff)
+            gate = dot_nn(h2, w_in_ref[s, 0])
+            up = dot_nn(h2, w_in_ref[s, 1])
+            c = (2.0 / jnp.pi) ** 0.5
+            sq = gate * gate
+            t = jnp.tanh(c * gate * (1.0 + 0.044715 * sq))
+            half = 0.5 * (1.0 + t)
+            gelu = gate * half
+            act[:, cols] = gelu
+            slope[:, cols] = up * (
+                half + 0.5 * gate * (1.0 - t * t) * (c * (1.0 + 3 * 0.044715 * sq))
+            )
+            hidden = (gelu * up).astype(bf16)
+            hid_all[s, rows] = hidden
+            m += dot_nn(hidden, w_down_ref[s])
+        r_m = inverse_rms(m)
+        mixed_ref[...] = (x2 + m * r_m * gain_post).astype(bf16)
+        dm = rms_back(m, r_m, gain_post, e).astype(bf16)
+        dh2 = jnp.zeros((row_block, model), f32)
+        for s in range(shards):
+            cols = slice(s * ff, (s + 1) * ff)
+            dh = dot_nt(dm, w_down_ref[s])
+            dgate = (dh * slope[:, cols]).astype(bf16)
+            dup = (dh * act[:, cols]).astype(bf16)
+            dg_all[s, rows] = dgate
+            du_all[s, rows] = dup
+            dh2 += dot_nt(dgate, w_in_ref[s, 0]) + dot_nt(dup, w_in_ref[s, 1])
+        dx2 = e + rms_back(x2, r_x2, gain_pre, dh2)
+        dx2_ref[...] = dx2
+        db = rms_back(branch, r_branch, gain_attn, dx2).astype(bf16)
+        do_ref[...] = dot_nt(db, w_out_ref[...]).astype(bf16)
+        h2_all[rows] = h2
+        dm_all[rows] = dm
+        db_all[rows] = db
+        for s in range(shards):
+            o_all[s, rows] = o[:, s * heads : (s + 1) * heads]
+
+        @pl.when(step == 0)
+        def _():
+            dgains_ref[...] = jnp.zeros_like(dgains_ref)
+
+        dgains_ref[0:1] += jnp.sum(dx2 * branch * r_branch, axis=0, keepdims=True)
+        dgains_ref[1:2] += jnp.sum(dh2 * x2 * r_x2, axis=0, keepdims=True)
+        dgains_ref[2:3] += jnp.sum(e * m * r_m, axis=0, keepdims=True)
+
+    @pl.when(step >= blocks)
+    def _():
+        s = step - blocks
+        h2_t = h2_all[...].T
+        ffn_ref[0, 0:model] = dot_nn(h2_t, dg_all[s]).astype(bf16)
+        ffn_ref[0, model : 2 * model] = dot_nn(h2_t, du_all[s]).astype(bf16)
+        ffn_ref[0, 2 * model : 3 * model] = dot_nn(dm_all[...].T, hid_all[s]).astype(bf16)
+        out_ref[0] = dot_nn(db_all[...].T, o_all[s]).astype(bf16)
+
+
+def middle(x, attended, out_grad, w_out, w_in, w_down, gains):
+    rows, model = x.shape
+    inner = attended.shape[1]
+    shards, _, _, ff = w_in.shape
+    blocks = rows // row_block
+    heads = inner // shards
+
+    def row_spec(width):
+        return pl.BlockSpec((row_block, width), lambda i: (jnp.minimum(i, blocks - 1), 0))
+
+    def whole(shape):
+        return pl.BlockSpec(shape, lambda i: (0,) * len(shape), pipeline_mode=pl.Buffered(1))
+
+    def shard_spec(shape):
+        return pl.BlockSpec((1,) + shape, lambda i: (jnp.maximum(i - blocks, 0), 0, 0))
+
+    return pl.pallas_call(
+        partial(middle_kernel, blocks, shards),
+        grid=(blocks + shards,),
+        in_specs=[
+            row_spec(model), row_spec(inner), row_spec(model),
+            whole(w_out.shape), whole(w_in.shape), whole(w_down.shape), whole(gains.shape),
+        ],
+        out_specs=[
+            row_spec(model), row_spec(model), row_spec(inner),
+            shard_spec((3 * model, ff)), shard_spec((model, heads)),
+            pl.BlockSpec((8, model), lambda i: (0, 0)),
+        ],
+        out_shape=[
+            jax.ShapeDtypeStruct((rows, model), bf16),
+            jax.ShapeDtypeStruct((rows, model), f32),
+            jax.ShapeDtypeStruct((rows, inner), bf16),
+            jax.ShapeDtypeStruct((shards, 3 * model, ff), bf16),
+            jax.ShapeDtypeStruct((shards, model, heads), bf16),
+            jax.ShapeDtypeStruct((8, model), f32),
+        ],
+        scratch_shapes=[
+            pltpu.VMEM((row_block, shards * ff), f32),
+            pltpu.VMEM((row_block, shards * ff), f32),
+            pltpu.VMEM((rows, model), bf16),
+            pltpu.VMEM((rows, model), bf16),
+            pltpu.VMEM((rows, model), bf16),
+            pltpu.VMEM((shards, rows, heads), bf16),
+            pltpu.VMEM((shards, rows, ff), bf16),
+            pltpu.VMEM((shards, rows, ff), bf16),
+            pltpu.VMEM((shards, rows, ff), bf16),
+        ],
+        compiler_params=pltpu.CompilerParams(vmem_limit_bytes=vmem_most),
+        cost_estimate=pl.CostEstimate(
+            flops=2 * rows * model * 3 * (3 * shards * ff + inner),
+            bytes_accessed=30 << 20, transcendentals=rows * shards * ff,
+        ),
+        name="middle",
+    )(x, attended, out_grad, w_out, w_in, w_down, gains)
+
+
+def turn_kernel(ffn_ref, attn_ref, down_ref, out_ref):
+    down_ref[...] = ffn_ref[...].astype(f32).T
+    out_ref[...] = attn_ref[...].astype(f32).T
+
+
+def turn(ffn_part, attn_part):
+    return pl.pallas_call(
+        turn_kernel,
+        out_shape=[
+            jax.ShapeDtypeStruct(part.shape[::-1], f32) for part in (ffn_part, attn_part)
+        ],
+        compiler_params=pltpu.CompilerParams(vmem_limit_bytes=24 * 1024 * 1024),
+        name="turn",
+    )(ffn_part, attn_part)
 
 
 def score_block(queries, key_rows, allowed):
@@ -172,8 +349,8 @@
     w_qkv, w_out, w_ffin, w_ffout, gains_low = (
         lax.all_gather(qkv_weight.astype(jnp.bfloat16), "shard", axis=1, tiled=True),
         lax.all_gather(out_weight.astype(jnp.bfloat16), "shard", axis=0, tiled=True),
-        lax.all_gather(ff_in_weight.astype(jnp.bfloat16), "shard", axis=2, tiled=True),
-        lax.all_gather(ff_out_weight.astype(jnp.bfloat16), "shard", axis=0, tiled=True),
+        lax.all_gather(ff_in_weight.astype(jnp.bfloat16), "shard", axis=0),
+        lax.all_gather(ff_out_weight.astype(jnp.bfloat16), "shard", axis=0),
         lax.all_gather(norm_gains.astype(jnp.bfloat16), "shard", axis=0, tiled=True),
     )
     gain_in, gain_attn, gain_pre, gain_post, gain_query, gain_key = split_gains(
@@ -214,61 +391,25 @@
         preferred_element_type=jnp.float32,
     )
     attended_low = attended.reshape(row_count, QH * HEAD).astype(jnp.bfloat16)
-    branch = jnp.dot(attended_low, w_out, preferred_element_type=jnp.float32)
-    middle = tokens + rms_scale(branch, gain_attn)
-    normed_two = rms_scale(middle, gain_pre).astype(jnp.bfloat16)
-    gate_proj = jnp.dot(normed_two, w_ffin[0], preferred_element_type=jnp.float32)
-    upward = jnp.dot(normed_two, w_ffin[1], preferred_element_type=jnp.float32)
-    hidden = (jax.nn.gelu(gate_proj, approximate=True) * upward).astype(jnp.bfloat16)
-    branch_two = jnp.dot(hidden, w_ffout, preferred_element_type=jnp.float32)
-    mixed = (
-        (middle + rms_scale(branch_two, gain_post))
-        .astype(jnp.bfloat16)
-        .reshape(seqs_here, span_rows, model_width)
-    )
-    cotangent = out_grad.astype(jnp.float32).reshape(row_count, model_width)
-    post_back = jax.vjp(rms_scale, branch_two, gain_post)[1]
-    grad_branch_two, grad_gain_post = post_back(cotangent)
-    grad_ffn_low = grad_branch_two.astype(jnp.bfloat16)
-    grad_hidden = jnp.einsum("nd,fd->nf", grad_ffn_low, w_ffout, preferred_element_type=jnp.float32)
-    gelu_back = jax.vjp(
-        lambda gate_in, up_in: jax.nn.gelu(gate_in, approximate=True) * up_in, gate_proj, upward
-    )[1]
-    grad_gate, grad_up = gelu_back(grad_hidden)
-    grad_gate_low = grad_gate.astype(jnp.bfloat16)
-    grad_up_low = grad_up.astype(jnp.bfloat16)
     shards = lax.axis_size("shard")
     low_dot = partial(jnp.einsum, preferred_element_type=jnp.float32)
-    ffn_parts = jnp.concatenate(
-        [
-            part.astype(jnp.bfloat16).reshape(model_width, shards, -1).swapaxes(0, 1)
-            for part in (
-                low_dot("nd,nf->df", normed_two, grad_gate_low),
-                low_dot("nd,nf->df", normed_two, grad_up_low),
-                low_dot("nd,nf->df", grad_ffn_low, hidden),
-            )
-        ],
-        axis=1,
-    )
-    grad_gate_low, grad_up_low, ffn_parts = together(grad_gate_low, grad_up_low, ffn_parts)
+    mixed, grad_middle, grad_attended, ffn_parts, out_parts, grad_three = middle(
+        block_input.reshape(row_count, model_width),
+        attended_low,
+        out_grad.reshape(row_count, model_width),
+        w_out,
+        w_ffin,
+        w_ffout,
+        jnp.stack([gain_attn, gain_pre, gain_post]),
+    )
+    mixed = mixed.reshape(block_input.shape)
+    grad_gain_attn, grad_gain_pre, grad_gain_post = grad_three[0], grad_three[1], grad_three[2]
+    grad_attended = grad_attended.reshape(seqs_here, span_rows, QH, HEAD)
     ffn_steps = reduce_steps(ffn_parts)
     ffn_sum = next(ffn_steps)
-    grad_normed_two = jnp.einsum(
-        "nf,df->nd", grad_gate_low, w_ffin[0], preferred_element_type=jnp.float32
-    ) + jnp.einsum("nf,df->nd", grad_up_low, w_ffin[1], preferred_element_type=jnp.float32)
-    pre_back = jax.vjp(rms_scale, middle, gain_pre)[1]
-    grad_middle_ffn, grad_gain_pre = pre_back(grad_normed_two)
-    grad_middle = cotangent + grad_middle_ffn
-    attn_back = jax.vjp(rms_scale, branch, gain_attn)[1]
-    grad_branch, grad_gain_attn = attn_back(grad_middle)
-    grad_attn_low = grad_branch.astype(jnp.bfloat16)
-    grad_attended = jnp.einsum(
-        "nd,kd->nk", grad_attn_low, w_out, preferred_element_type=jnp.float32
-    )
-    grad_attended = grad_attended.astype(jnp.bfloat16).reshape(seqs_here, span_rows, QH, HEAD)
-    grad_attended, ffn_sum = together(grad_attended, ffn_sum)
+    scores_back = score_block(queries, all_keys, allowed)
+    scores_back, ffn_sum = together(scores_back, ffn_sum)
     ffn_sum = advance(ffn_steps, ffn_sum)
-    scores_back = score_block(queries, all_keys, allowed)
     probs_back = jnp.exp(scores_back - log_total)
     grad_values = jnp.einsum(
         "shqk,sqhd->skd",
@@ -307,20 +448,6 @@
     grad_project_low = grad_project.reshape(row_count, -1).astype(jnp.bfloat16)
     grad_project_low, ffn_sum = together(grad_project_low, ffn_sum)
     ffn_sum = advance(ffn_steps, ffn_sum)
-    attn_parts = jnp.concatenate(
-        [
-            part.astype(jnp.bfloat16).reshape(model_width, shards, -1).swapaxes(0, 1)
-            for part in (
-                low_dot("nd,nk->dk", normed, grad_project_low),
-                low_dot("nd,nk->dk", grad_attn_low, attended_low),
-            )
-        ],
-        axis=2,
-    )
-    grad_project_low, attn_parts = together(grad_project_low, attn_parts)
-    attn_steps = reduce_steps(attn_parts)
-    attn_total = finish(attn_steps, next(attn_steps))
-    ffn_total = finish(ffn_steps, ffn_sum)
     grad_normed = jnp.einsum(
         "nk,dk->nd", grad_project_low, w_qkv, preferred_element_type=jnp.float32
     )
@@ -339,24 +466,36 @@
             grad_gain_key,
         ]
     )
+    qkv_here = qkv_weight.shape[1]
+    gains_here = norm_gains.shape[0]
+    gain_rows = jnp.pad(
+        grad_gains.astype(jnp.bfloat16).reshape(shards, gains_here // 128, 128),
+        ((0, 0), (0, 64 - gains_here // 128), (0, model_width - 128)),
+    )
+    qkv_parts = low_dot("nd,nk->dk", normed, grad_project_low).astype(jnp.bfloat16)
+    qkv_parts = qkv_parts.reshape(model_width, shards, -1).swapaxes(0, 1)
+    attn_parts = jnp.concatenate(
+        [jnp.concatenate([qkv_parts, out_parts], axis=2), gain_rows], axis=1
+    )
+    attn_steps = reduce_steps(attn_parts)
+    attn_total = finish(attn_steps, next(attn_steps))
+    ffn_total = finish(ffn_steps, ffn_sum)
     masters = (qkv_weight, out_weight, ff_in_weight, ff_out_weight, norm_gains)
     moments = (qkv_moment, out_moment, ff_in_moment, ff_out_moment, gains_moment)
     squares = (qkv_square, out_square, ff_in_square, ff_out_square, gains_square)
     step_rates = (rate_matrix, rate_matrix, rate_matrix, rate_matrix, rate_gain)
     decays = (decay_matrix, decay_matrix, decay_matrix, decay_matrix, 0.0)
-    gains_here = norm_gains.shape[0]
-    gains_total = lax.dynamic_slice_in_dim(
-        lax.psum(grad_gains, ("shard", "seq")), lax.axis_index("shard") * gains_here, gains_here
-    )
-    qkv_here = qkv_weight.shape[1]
-    attn_total, ffn_total = together(attn_total, ffn_total)
-    down_total, out_total = together(ffn_total[2 * model_width :].T, attn_total[:, qkv_here:].T)
+    down_total, out_total = turn(
+        ffn_total[2 * model_width :], attn_total[:model_width, qkv_here:]
+    )
     totals = (
-        attn_total[:, :qkv_here].astype(jnp.float32),
-        out_total.astype(jnp.float32),
+        attn_total[:model_width, :qkv_here].astype(jnp.float32),
+        out_total,
         ffn_total[: 2 * model_width].reshape(ff_in_weight.shape).astype(jnp.float32),
-        down_total.astype(jnp.float32),
-        gains_total,
+        down_total,
+        attn_total[model_width : model_width + gains_here // 128, :128]
+        .reshape(gains_here)
+        .astype(jnp.float32),
     )
     results = [
         adam_step(

time: 495 us -> 427 us (0.86)
  matrix products: 114 us -> 54.2 us
  Pallas kernels: 0 us -> 52 us
  blocking collectives: 56.8 us -> 5.2 us
  waiting for transfers between devices: 88.6 us -> 126 us
  local copies, waits for them, and re-layouts: 72.4 us -> 35.9 us
  other arithmetic: 102 us -> 95.3 us
    dot_general x13 -> x1, matrix products: 62.6 us -> 2.27 us  [on_device(): low_dot('nd,nk->dk', normed, grad_project_low).astype(jnp.bfloat16)]
    pallas_call x0 -> x2, Pallas kernels: none -> 52 us  [the longest x1 51.6 us: middle(): pl.pallas_call(partial(middle_kernel, blocks, shards), grid=(blocks + sha...]
    psum x1 -> x0, blocking collectives: 51.6 us -> none  [on_device(): lax.psum(grad_gains, ('shard', 'seq'))]
    unnamed x194 -> x104, local copies, waits for them, and re-layouts: 44.8 us -> 8.38 us
    all_gather x2, waiting for transfers between devices: 0.01 us -> 25.3 us  [the longest x1 25.3 us: on_device(): lax.all_gather(ff_in_weight.astype(jnp.bfloat16), 'shard', axis=0)]
    ppermute x16, waiting for transfers between devices: 63.6 us -> 84.3 us  [swap_bit(): lax.ppermute(block, axis, [(i, i ^ 1 << bit) for i in range(lax.axis_size...]
    ppermute x5, waiting for transfers between devices: 17.9 us -> 12 us  [from_behind(): return lax.ppermute(block, axis, route)]
    sub x5, other arithmetic: 17.4 us -> 11.6 us  [adam_step(): weight - step_rate * (moment_hat / (jnp.sqrt(square_hat) + adam_eps) + de...]
  transfers between devices with their start and end apart: 25 -> 25, of which waited for: 14 -> 16; matrix products, arithmetic and copies ran while one was open for 37% -> 33% of each run, Pallas kernels for 0% -> 0%
where the time goes in v2:
time: 427 us; the launch traced here: 421 us
  waiting for transfers between devices  126 us (30%)
  other arithmetic  95.3 us (22%)
  matrix products  54.2 us (13%)
  Pallas kernels  52 us (12%)
  starting transfers between devices  37 us (9%)
  local copies, waits for them, and re-layouts  35.9 us (8%)
  between operations  15.1 us (4%)
  blocking collectives  5.2 us (1%)
    ppermute x16, waiting for transfers between devices, swap_bit(): lax.ppermute(block, axis, [(i, i ^ 1 << bit) for i in range(lax.axis_size...  84.3 us
    pallas_call x1, Pallas kernels, middle(): pl.pallas_call(partial(middle_kernel, blocks, shards), grid=(blocks + sha...  51.6 us
    all_gather x1, waiting for transfers between devices, on_device(): lax.all_gather(ff_in_weight.astype(jnp.bfloat16), 'shard', axis=0)  25.3 us
    sub x1, other arithmetic, on_device(): grad_scores = (probs_back * (grad_probs - inner_sum)).astype(jnp.bfloat16)  22.6 us
    ppermute x16, starting transfers between devices, swap_bit(): lax.ppermute(block, axis, [(i, i ^ 1 << bit) for i in range(lax.axis_size...  21.2 us
    ppermute x5, starting transfers between devices, from_behind(): return lax.ppermute(block, axis, route)  15.6 us
    convert_element_type x10, other arithmetic, halve(): (kept.astype(jnp.float32) + came.astype(jnp.float32)).astype(jnp.bfloat16)  14.3 us
    ppermute x5, waiting for transfers between devices, from_behind(): return lax.ppermute(block, axis, route)  12 us
  transfers between devices with their start and end apart: 25, of which 16 were waited for; matrix products, arithmetic and copies ran while one was open for 33% of the time, Pallas kernels for 0%

profile of v2, /device:TPU:0, one launch (start us, length us, event | category | flops | bytes accessed | tf_op | source)
XLA Modules:
  0.0 420.6 jit_solution(9442899788422954099)
XLA Ops:
  13.8 4.9 %collective-permute-start.1 = (s32[2,512]{1,0:T(2,128)S(1)}, s32[2,512]{1,0:T(2,128)S(1)}, u32[]{:S(2)}, u32[]{:S(2)}) collective-permute-start(s32[2,512]{1,0:T(2,128)S(1)} %copy-done.41), channel_id=1, source_target_pairs={{0,4},{4,8},{8,12},{12,16},{16,20},{20,24},{24,28},{1,5},{5,9},{9,... | collective-permute-start | bytes 12296 | tf_op jit(solution)/shard_map/ppermute | solution.py:31
  22.0 5.2 %all-gather.2 = bf16[4,1,768]{2,1,0:T(2,128)(2,1)S(1)} all-gather(bf16[1,1,768]{2,1,0:T(2,128)(2,1)S(1)} %reshape.306), channel_id=1, replica_groups=mesh['seq'=8,'shard'=4] {'shard'}, dimensions={0}, use_global_device_ids=true | all-gather | bytes 7680 | tf_op jit(solution)/shard_map/all_gather | solution.py:354
  48.9 4.6 %collective-permute-start.2 = (bf16[2,512,256]{2,1,0:T(8,128)(2,1)}, bf16[2,512,256]{2,1,0:T(8,128)(2,1)}, u32[]{:S(2)}, u32[]{:S(2)}) collective-permute-start(bf16[2,512,256]{2,1,0:T(8,128)(2,1)} %pad_maximum_fusion.5), channel_id=1, source_target_pairs={{0,4},{4,8},{8,12},{12,16},{16,20},{20,24},{24,28},{1,5},{5,9},{9,... | collective-permute-start | bytes 1572872 | tf_op jit(solution)/shard_map/ppermute | solution.py:31
  53.5 5.6 %reshape.280 = f32[2,512,4,256]{3,2,1,0:T(4,128)} reshape(f32[2,512,1024]{2,1,0:T(8,128)} %slice.114) | data formatting | bytes 8388608 | tf_op jit(solution)/shard_map/reshape | solution.py:123
  68.1 8.5 %fusion.93 = (f32[2,4,512]{2,1,0:T(4,128)S(1)}, f32[2,4,512,1024]{2,3,1,0:T(8,128)}) fusion(bf16[2,512,4,128]{3,1,2,0:T(8,128)(2,1)S(1)} %get-tuple-element.72, bf16[2,512,4,128]{3,1,2,0:T(8,128)(2,1)S(1)} %get-tuple-element.71, bf16[2,512,128]{2,1,0:T(8,128)(2,1)S(1)} %get-tuple-element.79, bf16[2,512,128]{2,1,0:T(8,128)(2,1)S(1)} %get-tuple-element.78, ...), kind=kOutput, calls=%fused_computation.201 | convolution fusion | flops 2167402496 | bytes 20987904 | tf_op jit(solution)/shard_map/sqhd,skd->shqk/dot_general | solution.py:309
  76.6 8.1 %fusion.3 = f32[2,4,512]{2,1,0:T(4,128)S(1)} fusion(f32[2,4,512,1024]{2,3,1,0:T(8,128)} %get-tuple-element.34, f32[2,4,512]{2,1,0:T(4,128)S(1)} %get-tuple-element.100), kind=kLoop, calls=%fused_computation.9 | loop fusion | flops 8384512 | bytes 16809984 | tf_op jit(solution)/shard_map/reduce_sum | solution.py:384
  84.7 10.4 %convert_bitcast_fusion = bf16[2,512,4,256]{1,3,2,0:T(8,128)(2,1)} fusion(f32[2,4,512,1024]{2,3,1,0:T(8,128)} %get-tuple-element.34, f32[2,4,512]{2,1,0:T(4,128)S(1)} %fusion.3, f32[2,4,512]{2,1,0:T(4,128)S(1)} %get-tuple-element.100, bf16[2,512,256]{2,1,0:T(8,128)(2,1)S(1)} %slice.174, bf16[2,512,256]{2,1,0:T(8,128)(2,1)S(1)} %collective-permute-done), kind=kOutput, calls=%fused_computation.64 | convolution fusion | flops 2163212288 | bytes 19955712 | tf_op jit(solution)/shard_map/shqk,skd->sqhd/dot_general | solution.py:387
  100.0 25.3 %all-gather.12.cloned.1.call-done = bf16[8,640,512]{2,1,0:T(8,128)(2,1)} async-done(((bf16[2,640,512]{2,1,0:T(8,128)(2,1)}), bf16[8,640,512]{2,1,0:T(8,128)(2,1)}) %all-gather.12.cloned.1.call-update) | async-done | bytes 5242896 | tf_op jit(solution)/shard_map/all_gather | solution.py:352
  125.4 51.6 %middle.1 = (bf16[1024,640]{1,0:T(8,128)(2,1)}, f32[1024,640]{1,0:T(8,128)}, bf16[1024,1024]{1,0:T(8,128)(2,1)}, bf16[4,1920,512]{2,1,0:T(8,128)(2,1)}, bf16[4,640,256]{2,1,0:T(8,128)(2,1)}, /*index=5*/f32[8,640]{1,0:T(8,128)}) custom-call(bf16[1024,640]{1,0:T(8,128)(2,1)} %bitcast.179, bf16[1024,1024]{1,0:T(8,128)(2,1)} %bitcast.186, ...), custom_call_target="tpu_custom_call" | custom-call | flops 28185722880 | bytes 31457280 | tf_op jit(solution)/shard_map/middle/pallas_call | solution.py:252
  185.2 8.2 %fusion.36 = f32[2,1024,512,4]{2,1,3,0:T(8,128)} fusion(bf16[2,512,4,256]{3,2,1,0:T(4,128)(2,1)S(1)} %reshape.284, bf16[2,512,256]{2,1,0:T(8,128)(2,1)S(1)} %copy-done.20, bf16[2,512,256]{2,1,0:T(8,128)(2,1)S(1)} %copy-done.39), kind=kOutput, calls=%fused_computation.78 | convolution fusion | flops 2149580800 | bytes 19922944 | tf_op jit(solution)/shard_map/sqhd,skd->shqk/dot_general | solution.py:420
  193.4 4.4 %fusion.9 = bf16[2,1920,512]{2,1,0:T(8,128)(2,1)S(1)} fusion(bf16[2,1920,512]{2,1,0:T(8,128)(2,1)} %collective-permute-done.3, bf16[2,2,1920,512]{3,2,1,0:T(8,128)(2,1)} %bitcast.174, s32[]{:T(128)S(6)} %select_n.128), kind=kLoop, calls=%fused_computation.15 | loop fusion | flops 7864320 | bytes 11796484 | tf_op jit(solution)/shard_map/convert_element_type | solution.py:47
  199.6 9.4 %fusion.39 = f32[2,1024,256]{2,1,0:T(8,128)} fusion(bf16[2,512,4,256]{3,2,1,0:T(4,128)(2,1)S(1)} %reshape.284, f32[2,4,512,1024]{2,3,1,0:T(8,128)} %get-tuple-element.34, f32[2,4,512]{2,1,0:T(4,128)S(1)} %bitcast.195), kind=kOutput, calls=%fused_computation.83 | convolution fusion | flops 2155872256 | bytes 20987904 | tf_op jit(solution)/shard_map/shqk,sqhd->skd/dot_general | solution.py:414
  212.5 22.6 %fusion.2 = bf16[2,4,512,1024]{2,3,1,0:T(8,128)(2,1)S(1)} fusion(f32[2,1024,512,4]{2,1,3,0:T(8,128)} %fusion.36, f32[2,4,512,1024]{2,3,1,0:T(8,128)} %get-tuple-element.34, f32[2,4,512]{2,1,0:T(4,128)S(1)} %bitcast.196), kind=kOutput, calls=%fused_computation.4 | output fusion | flops 25170944 | bytes 41959424 | tf_op jit(solution)/shard_map/sub | solution.py:424
  236.2 8.3 %collective-permute-done.5 = bf16[1,1920,512]{2,1,0:T(8,128)(2,1)} collective-permute-done((bf16[1,1920,512]{2,1,0:T(8,128)(2,1)}, bf16[1,1920,512]{2,1,0:T(8,128)(2,1)}, u32[]{:S(2)}, u32[]{:S(2)}) %collective-permute-start.5) | collective-permute-done | bytes 1966112 | tf_op jit(solution)/shard_map/ppermute | solution.py:35
  249.1 4.5 %multiply_bitcast_fusion = f32[2,512,4,256]{3,1,2,0:T(8,128)S(1)} fusion(bf16[2,4,512,1024]{2,3,1,0:T(8,128)(2,1)S(1)} %fusion.2, bf16[2,512,128]{2,1,0:T(8,128)(2,1)S(1)} %copy-done.33, bf16[2,512,128]{2,1,0:T(8,128)(2,1)S(1)} %copy-done.31, bf16[2,512,256]{2,1,0:T(8,128)(2,1)} %collective-permute-done.2), kind=kOutput, calls=%fused_computation.28 | convolution fusion | flops 2151677952 | bytes 13631488 | tf_op jit(solution)/shard_map/shqk,skd->sqhd/dot_general | solution.py:427
  264.0 10.1 %collective-permute-done.6 = bf16[2,512,256]{2,1,0:T(8,128)(2,1)S(1)} collective-permute-done((bf16[2,512,256]{2,1,0:T(8,128)(2,1)S(1)}, bf16[2,512,256]{2,1,0:T(8,128)(2,1)S(1)}, u32[]{:S(2)}, u32[]{:S(2)}) %collective-permute-start.6) | collective-permute-done | bytes 524320 | tf_op jit(solution)/shard_map/ppermute | solution.py:31
  280.1 13.5 %collective-permute-done.7 = bf16[960,512]{1,0:T(8,128)(2,1)S(1)} collective-permute-done((bf16[960,512]{1,0:T(8,128)(2,1)S(1)}, bf16[960,512]{1,0:T(8,128)(2,1)S(1)}, u32[]{:S(2)}, u32[]{:S(2)}) %collective-permute-start.7) | collective-permute-done | bytes 983072 | tf_op jit(solution)/shard_map/ppermute | solution.py:35
  315.7 6.8 %collective-permute-done.16 = bf16[480,512]{1,0:T(8,128)(2,1)} collective-permute-done((bf16[480,512]{1,0:T(8,128)(2,1)}, bf16[480,512]{1,0:T(8,128)(2,1)}, u32[]{:S(2)}, u32[]{:S(2)}) %collective-permute-start.16) | collective-permute-done | bytes 491552 | tf_op jit(solution)/shard_map/ppermute | solution.py:35
  327.1 11.4 %collective-permute-done.17 = bf16[240,512]{1,0:T(8,128)(2,1)} collective-permute-done((bf16[240,512]{1,0:T(8,128)(2,1)S(1)}, bf16[240,512]{1,0:T(8,128)(2,1)}, u32[]{:S(2)}, u32[]{:S(2)}) %collective-permute-start.17) | collective-permute-done | bytes 245792 | tf_op jit(solution)/shard_map/ppermute | solution.py:35
  343.6 9.2 %collective-permute-done.18 = bf16[240,512]{1,0:T(8,128)(2,1)S(1)} collective-permute-done((bf16[240,512]{1,0:T(8,128)(2,1)S(1)}, bf16[240,512]{1,0:T(8,128)(2,1)S(1)}, u32[]{:S(2)}, u32[]{:S(2)}) %collective-permute-start.18) | collective-permute-done | bytes 245792 | tf_op jit(solution)/shard_map/ppermute | solution.py:35
  357.4 9.5 %collective-permute-done.19 = bf16[480,512]{1,0:T(8,128)(2,1)S(1)} collective-permute-done((bf16[480,512]{1,0:T(8,128)(2,1)S(1)}, bf16[480,512]{1,0:T(8,128)(2,1)S(1)}, u32[]{:S(2)}, u32[]{:S(2)}) %collective-permute-start.19) | collective-permute-done | bytes 491552 | tf_op jit(solution)/shard_map/ppermute | solution.py:35
  376.9 12.7 %collective-permute-done.20 = bf16[960,512]{1,0:T(8,128)(2,1)S(1)} collective-permute-done((bf16[960,512]{1,0:T(8,128)(2,1)S(1)}, bf16[960,512]{1,0:T(8,128)(2,1)S(1)}, u32[]{:S(2)}, u32[]{:S(2)}) %collective-permute-start.20) | collective-permute-done | bytes 983072 | tf_op jit(solution)/shard_map/ppermute | solution.py:35
  390.9 5.3 %collective-permute-done.14 = bf16[176,640]{1,0:T(8,128)(2,1)S(1)} collective-permute-done((bf16[176,640]{1,0:T(8,128)(2,1)S(1)}, bf16[176,640]{1,0:T(8,128)(2,1)S(1)}, u32[]{:S(2)}, u32[]{:S(2)}) %collective-permute-start.14) | collective-permute-done | bytes 225312 | tf_op jit(solution)/shard_map/ppermute | solution.py:35
  398.2 4.7 %multiply_subtract_fusion = (f32[2,640,512]{2,1,0:T(8,128)}, f32[2,640,512]{2,1,0:T(8,128)}, f32[2,640,512]{2,1,0:T(8,128)}) fusion(f32[2,640,512]{2,1,0:T(8,128)S(1)} %copy-done.4, bf16[2,640,512]{2,1,0:T(8,128)(2,1)S(1)} %bitcast.178, f32[2,640,512]{2,1,0:T(8,128)S(1)} %copy-done.17, f32[2,640,512]{2,1,0:T(8,128)S(1)} %copy-done.18), kind=kLoop, calls=%fused_computation.59 | loop fusion | flops 10485760 | bytes 17039360 | tf_op jit(solution)/shard_map/sub | solution.py:320
  (247 shorter events, 140.6 us)
Async XLA Ops:
  7.2 27.6 %all-gather.8.cloned.1.call-start = ((), (), s32[]{:S(2)}) async-start(), calls=%async_computation | async-start | bytes 2457600 | tf_op jit(solution)/shard_map/all_gather | solution.py:350
  9.5 90.5 %all-gather.10.cloned.1.call-start = ((), (), s32[]{:S(2)}) async-start(), calls=%async_computation.1 | async-start | bytes 1638400 | tf_op jit(solution)/shard_map/all_gather | solution.py:351
  11.4 88.6 %all-gather.14.cloned.1.call-start = ((), (), s32[]{:S(2)}) async-start(), calls=%async_computation.3 | async-start | bytes 3276800 | tf_op jit(solution)/shard_map/all_gather | solution.py:353
  13.7 111.7 %all-gather.12.cloned.1.call-start = ((), (), s32[]{:S(2)}) async-start(), calls=%async_computation.2 | async-start | bytes 6553600 | tf_op jit(solution)/shard_map/all_gather | solution.py:352
  13.8 15.1 %collective-permute-start.1 = (s32[2,512]{1,0:T(2,128)S(1)}, s32[2,512]{1,0:T(2,128)S(1)}, u32[]{:S(2)}, u32[]{:S(2)}) collective-permute-start(s32[2,512]{1,0:T(2,128)S(1)} %copy-done.41), channel_id=1, source_target_pairs={{0,4},{4,8},{8,12},{12,16},{16,20},{20,24},{24,28},{1,5},{5,9},{9,... | collective-permute-start | bytes 12296 | tf_op jit(solution)/shard_map/ppermute | solution.py:31
  41.8 42.9 %collective-permute-start = (bf16[2,512,256]{2,1,0:T(8,128)(2,1)S(1)}, bf16[2,512,256]{2,1,0:T(8,128)(2,1)S(1)}, u32[]{:S(2)}, u32[]{:S(2)}) collective-permute-start(bf16[2,512,256]{2,1,0:T(8,128)(2,1)S(1)} %slice.174), channel_id=1, source_target_pairs={{0,4},{4,8},{8,12},{12,16},{16,20},{20,24},{24,28},{1,5},{5,9},{9,... | collective-permute-start | bytes 1572872 | tf_op jit(solution)/shard_map/ppermute | solution.py:31
  48.9 19.2 %collective-permute-start.2 = (bf16[2,512,256]{2,1,0:T(8,128)(2,1)}, bf16[2,512,256]{2,1,0:T(8,128)(2,1)}, u32[]{:S(2)}, u32[]{:S(2)}) collective-permute-start(bf16[2,512,256]{2,1,0:T(8,128)(2,1)} %pad_maximum_fusion.5), channel_id=1, source_target_pairs={{0,4},{4,8},{8,12},{12,16},{16,20},{20,24},{24,28},{1,5},{5,9},{9,... | collective-permute-start | bytes 1572872 | tf_op jit(solution)/shard_map/ppermute | solution.py:31
  181.3 12.1 %collective-permute-start.3 = (bf16[2,1920,512]{2,1,0:T(8,128)(2,1)}, bf16[2,1920,512]{2,1,0:T(8,128)(2,1)}, u32[]{:S(2)}, u32[]{:S(2)}) collective-permute-start(bf16[2,1920,512]{2,1,0:T(8,128)(2,1)} %dynamic-slice_bitcast_fusion), channel_id=1, source_target_pairs={{0,1},{1,0},{2,3},{3,2},{4,5},{5,4},{6,7},{7,6},{8,9},{9,8},{10,11... | collective-permute-start | bytes 11796488 | tf_op jit(solution)/shard_map/ppermute | solution.py:35
  199.2 45.3 %collective-permute-start.5 = (bf16[1,1920,512]{2,1,0:T(8,128)(2,1)}, bf16[1,1920,512]{2,1,0:T(8,128)(2,1)}, u32[]{:S(2)}, u32[]{:S(2)}) collective-permute-start(bf16[1,1920,512]{2,1,0:T(8,128)(2,1)} %constant_dynamic-slice_fusion.1), channel_id=1, source_target_pairs={{0,2},{1,3},{2,0},{3,1},{4,6},{5,7},{6,4},{7,5},{8,10},{9,11},{10,... | collective-permute-start | bytes 5898248 | tf_op jit(solution)/shard_map/ppermute | solution.py:35
  211.1 24.0 %collective-permute-start.4 = (bf16[2,512,256]{2,1,0:T(8,128)(2,1)}, bf16[2,512,256]{2,1,0:T(8,128)(2,1)}, u32[]{:S(2)}, u32[]{:S(2)}) collective-permute-start(bf16[2,512,256]{2,1,0:T(8,128)(2,1)} %slice.173), channel_id=1, source_target_pairs={{4,0},{8,4},{12,8},{16,12},{20,16},{24,20},{28,24},{5,1},{9,5},{13... | collective-permute-start | bytes 1572872 | tf_op jit(solution)/shard_map/ppermute | solution.py:31
  257.3 16.8 %collective-permute-start.6 = (bf16[2,512,256]{2,1,0:T(8,128)(2,1)S(1)}, bf16[2,512,256]{2,1,0:T(8,128)(2,1)S(1)}, u32[]{:S(2)}, u32[]{:S(2)}) collective-permute-start(bf16[2,512,256]{2,1,0:T(8,128)(2,1)S(1)} %slice.172), channel_id=1, source_target_pairs={{4,0},{8,4},{12,8},{16,12},{20,16},{24,20},{28,24},{5,1},{9,5},{13... | collective-permute-start | bytes 1572872 | tf_op jit(solution)/shard_map/ppermute | solution.py:31
  261.2 32.3 %collective-permute-start.7 = (bf16[960,512]{1,0:T(8,128)(2,1)S(1)}, bf16[960,512]{1,0:T(8,128)(2,1)S(1)}, u32[]{:S(2)}, u32[]{:S(2)}) collective-permute-start(bf16[960,512]{1,0:T(8,128)(2,1)S(1)} %dynamic-slice_bitcast_fusion.2), channel_id=1, source_target_pairs={{0,4},{4,0},{8,12},{12,8},{16,20},{20,16},{24,28},{28,24},{1,5},{5... | collective-permute-start | bytes 2949128 | tf_op jit(solution)/shard_map/ppermute | solution.py:35
  308.5 13.9 %collective-permute-start.16 = (bf16[480,512]{1,0:T(8,128)(2,1)}, bf16[480,512]{1,0:T(8,128)(2,1)}, u32[]{:S(2)}, u32[]{:S(2)}) collective-permute-start(bf16[480,512]{1,0:T(8,128)(2,1)} %dynamic-slice_bitcast_fusion.3), channel_id=1, source_target_pairs={{0,8},{4,12},{8,0},{12,4},{16,24},{20,28},{24,16},{28,20},{1,9},{5... | collective-permute-start | bytes 1474568 | tf_op jit(solution)/shard_map/ppermute | solution.py:35
  315.3 24.5 %collective-permute-start.9 = (bf16[1,704,640]{2,1,0:T(8,128)(2,1)}, bf16[1,704,640]{2,1,0:T(8,128)(2,1)}, u32[]{:S(2)}, u32[]{:S(2)}) collective-permute-start(bf16[1,704,640]{2,1,0:T(8,128)(2,1)} %constant_dynamic-slice_fusion), channel_id=1, source_target_pairs={{0,2},{1,3},{2,0},{3,1},{4,6},{5,7},{6,4},{7,5},{8,10},{9,11},{10,... | collective-permute-start | bytes 2703368 | tf_op jit(solution)/shard_map/ppermute | solution.py:35
  324.6 13.9 %collective-permute-start.17 = (bf16[240,512]{1,0:T(8,128)(2,1)S(1)}, bf16[240,512]{1,0:T(8,128)(2,1)}, u32[]{:S(2)}, u32[]{:S(2)}) collective-permute-start(bf16[240,512]{1,0:T(8,128)(2,1)S(1)} %dynamic-slice_bitcast_fusion.5), channel_id=1, source_target_pairs={{0,16},{4,20},{8,24},{12,28},{16,0},{20,4},{24,8},{28,12},{1,17},{... | collective-permute-start | bytes 737288 | tf_op jit(solution)/shard_map/ppermute | solution.py:35
  339.7 13.2 %collective-permute-start.18 = (bf16[240,512]{1,0:T(8,128)(2,1)S(1)}, bf16[240,512]{1,0:T(8,128)(2,1)S(1)}, u32[]{:S(2)}, u32[]{:S(2)}) collective-permute-start(bf16[240,512]{1,0:T(8,128)(2,1)S(1)} %fusion.68), channel_id=1, source_target_pairs={{0,16},{4,20},{8,24},{12,28},{16,0},{20,4},{24,8},{28,12},{1,17},{... | collective-permute-start | bytes 737288 | tf_op jit(solution)/shard_map/ppermute | solution.py:35
  341.2 12.0 %collective-permute-start.10 = (bf16[352,640]{1,0:T(8,128)(2,1)S(1)}, bf16[352,640]{1,0:T(8,128)(2,1)S(1)}, u32[]{:S(2)}, u32[]{:S(2)}) collective-permute-start(bf16[352,640]{1,0:T(8,128)(2,1)S(1)} %dynamic-slice_bitcast_fusion.4), channel_id=1, source_target_pairs={{0,4},{4,0},{8,12},{12,8},{16,20},{20,16},{24,28},{28,24},{1,5},{5... | collective-permute-start | bytes 1351688 | tf_op jit(solution)/shard_map/ppermute | solution.py:35
  352.9 13.9 %collective-permute-start.19 = (bf16[480,512]{1,0:T(8,128)(2,1)S(1)}, bf16[480,512]{1,0:T(8,128)(2,1)S(1)}, u32[]{:S(2)}, u32[]{:S(2)}) collective-permute-start(bf16[480,512]{1,0:T(8,128)(2,1)S(1)} %pad_maximum_fusion.6), channel_id=1, source_target_pairs={{0,8},{4,12},{8,0},{12,4},{16,24},{20,28},{24,16},{28,20},{1,9},{5... | collective-permute-start | bytes 1474568 | tf_op jit(solution)/shard_map/ppermute | solution.py:35
  353.4 16.1 %collective-permute-start.11 = (bf16[176,640]{1,0:T(8,128)(2,1)S(1)}, bf16[176,640]{1,0:T(8,128)(2,1)S(1)}, u32[]{:S(2)}, u32[]{:S(2)}) collective-permute-start(bf16[176,640]{1,0:T(8,128)(2,1)S(1)} %dynamic-slice_bitcast_fusion.6), channel_id=1, source_target_pairs={{0,8},{4,12},{8,0},{12,4},{16,24},{20,28},{24,16},{28,20},{1,9},{5... | collective-permute-start | bytes 675848 | tf_op jit(solution)/shard_map/ppermute | solution.py:35
  367.1 22.5 %collective-permute-start.20 = (bf16[960,512]{1,0:T(8,128)(2,1)S(1)}, bf16[960,512]{1,0:T(8,128)(2,1)S(1)}, u32[]{:S(2)}, u32[]{:S(2)}) collective-permute-start(bf16[960,512]{1,0:T(8,128)(2,1)S(1)} %pad_maximum_fusion.4), channel_id=1, source_target_pairs={{0,4},{4,0},{8,12},{12,8},{16,20},{20,16},{24,28},{28,24},{1,5},{5... | collective-permute-start | bytes 2949128 | tf_op jit(solution)/shard_map/ppermute | solution.py:35
  369.5 6.7 %collective-permute-start.12 = (bf16[88,640]{1,0:T(8,128)(2,1)S(1)}, bf16[88,640]{1,0:T(8,128)(2,1)S(1)}, u32[]{:S(2)}, u32[]{:S(2)}) collective-permute-start(bf16[88,640]{1,0:T(8,128)(2,1)S(1)} %dynamic-slice_bitcast_fusion.7), channel_id=1, source_target_pairs={{0,16},{4,20},{8,24},{12,28},{16,0},{20,4},{24,8},{28,12},{1,17},{... | collective-permute-start | bytes 337928 | tf_op jit(solution)/shard_map/ppermute | solution.py:35
  376.3 13.8 %collective-permute-start.13 = (bf16[88,640]{1,0:T(8,128)(2,1)S(1)}, bf16[88,640]{1,0:T(8,128)(2,1)S(1)}, u32[]{:S(2)}, u32[]{:S(2)}) collective-permute-start(bf16[88,640]{1,0:T(8,128)(2,1)S(1)} %fusion.70), channel_id=1, source_target_pairs={{0,16},{4,20},{8,24},{12,28},{16,0},{20,4},{24,8},{28,12},{1,17},{... | collective-permute-start | bytes 337928 | tf_op jit(solution)/shard_map/ppermute | solution.py:35
  390.2 6.0 %collective-permute-start.14 = (bf16[176,640]{1,0:T(8,128)(2,1)S(1)}, bf16[176,640]{1,0:T(8,128)(2,1)S(1)}, u32[]{:S(2)}, u32[]{:S(2)}) collective-permute-start(bf16[176,640]{1,0:T(8,128)(2,1)S(1)} %pad_maximum_fusion.9), channel_id=1, source_target_pairs={{0,8},{4,12},{8,0},{12,4},{16,24},{20,28},{24,16},{28,20},{1,9},{5... | collective-permute-start | bytes 675848 | tf_op jit(solution)/shard_map/ppermute | solution.py:35
  396.3 8.8 %collective-permute-start.15 = (bf16[352,640]{1,0:T(8,128)(2,1)S(1)}, bf16[352,640]{1,0:T(8,128)(2,1)S(1)}, u32[]{:S(2)}, u32[]{:S(2)}) collective-permute-start(bf16[352,640]{1,0:T(8,128)(2,1)S(1)} %pad_maximum_fusion.7), channel_id=1, source_target_pairs={{0,4},{4,0},{8,12},{12,8},{16,20},{20,16},{24,28},{28,24},{1,5},{5... | collective-permute-start | bytes 1351688 | tf_op jit(solution)/shard_map/ppermute | solution.py:35
  (49 other events, 414.2 us)
Sparse Core Ops, SparseCore 0:
  10.2 24.5 all-gather.7
  36.9 18.1 all-gather.9
  57.3 25.5 all-gather.13
  84.9 40.4 all-gather.11

commit v3 on v2

--- a/solution.py
+++ b/solution.py
@@ -55,7 +55,10 @@
     for bit in range(bits_of("shard")):
         block = halve(block.reshape((-1, 2) + block.shape[1:]), "shard", bit, 1)
         block = yield block
-    block = block[0]
+    yield from seq_steps(block[0])
+
+
+def seq_steps(block):
     for bit in range(bits_of("seq")):
         block = halve(block.reshape((2, -1) + block.shape[1:]), "seq", bit, 0)
         block = yield block
@@ -119,15 +122,10 @@
     )
 
 
-def head_post(project, gain_query, gain_key, cos_table, sine_table):
-    queries = project[..., : QH * HEAD].reshape(project.shape[:-1] + (QH, HEAD))
-    key_rows = project[..., QH * HEAD : (QH + 1) * HEAD]
-    value_rows = project[..., (QH + 1) * HEAD :]
-    queries = rotate(
-        rms_scale(queries, gain_query), cos_table[..., None, :], sine_table[..., None, :]
-    )
-    key_rows = rotate(rms_scale(key_rows, gain_key), cos_table, sine_table)
-    return (queries, key_rows, value_rows)
+def head_post(pieces, gain_query, gain_key, cos_table, sine_table):
+    queries = [rotate(rms_scale(p, gain_query), cos_table, sine_table) for p in pieces[:QH]]
+    key_rows = rotate(rms_scale(pieces[QH], gain_key), cos_table, sine_table)
+    return (queries, key_rows, pieces[QH + 1])
 
 
 f32 = jnp.float32
@@ -153,14 +151,79 @@
     return r * gdy - v * (r * r * r) * jnp.mean(gdy * v, axis=-1, keepdims=True)
 
 
+def window_probs(block, head, q_ref, k_ref, seg_q_ref, seg_k_ref):
+    rows = slice(block * row_block, (block + 1) * row_block)
+    reach = slice(block * row_block, (block + 1) * row_block + WINDOW)
+    query = q_ref[0, rows, head * HEAD : (head + 1) * HEAD]
+    shape = (row_block, row_block + WINDOW)
+    ahead = lax.broadcasted_iota(jnp.int32, shape, 1) - lax.broadcasted_iota(jnp.int32, shape, 0)
+    same = seg_q_ref[0, rows] == seg_k_ref[0, :, reach]
+    allowed = (ahead > 0) & (ahead <= WINDOW) & same
+    scores = dot_nt(query, k_ref[0, reach]) * HEAD ** (-0.5)
+    scores = jnp.where(allowed, scores, masked_score)
+    terms = jnp.exp(scores - jnp.max(scores, axis=-1, keepdims=True))
+    return query, terms * (1.0 / jnp.sum(terms, axis=-1, keepdims=True))
+
+
+def attend_kernel(blocks, q_ref, k_ref, v_ref, seg_q_ref, seg_k_ref, o_ref):
+    for block in range(blocks):
+        rows = slice(block * row_block, (block + 1) * row_block)
+        reach = slice(block * row_block, (block + 1) * row_block + WINDOW)
+        for head in range(QH):
+            _, probs = window_probs(block, head, q_ref, k_ref, seg_q_ref, seg_k_ref)
+            out = dot_nn(probs.astype(bf16), v_ref[0, reach])
+            o_ref[0, rows, head * HEAD : (head + 1) * HEAD] = out.astype(bf16)
+
+
+def attend_back_kernel(
+    blocks, q_ref, k_ref, v_ref, seg_q_ref, seg_k_ref, do_ref, dq_ref, dk_ref, dv_ref
+):
+    dk_ref[...] = jnp.zeros_like(dk_ref)
+    dv_ref[...] = jnp.zeros_like(dv_ref)
+    for block in range(blocks):
+        rows = slice(block * row_block, (block + 1) * row_block)
+        reach = slice(block * row_block, (block + 1) * row_block + WINDOW)
+        for head in range(QH):
+            cols = slice(head * HEAD, (head + 1) * HEAD)
+            query, probs = window_probs(block, head, q_ref, k_ref, seg_q_ref, seg_k_ref)
+            do = do_ref[0, rows, cols]
+            dprobs = dot_nt(do, v_ref[0, reach])
+            inner = jnp.sum(probs * dprobs, axis=-1, keepdims=True)
+            dscores = (probs * (dprobs - inner)).astype(bf16)
+            dq_ref[0, rows, cols] = dot_nn(dscores, k_ref[0, reach]) * HEAD ** (-0.5)
+            dk_ref[0, reach] += dot_nn(dscores.T, query) * HEAD ** (-0.5)
+            dv_ref[0, reach] += dot_nn(probs.astype(bf16).T, do)
+
+
+def one_sequence(array):
+    return pl.BlockSpec((1,) + array.shape[1:], lambda i: (i,) + (0,) * (len(array.shape) - 1))
+
+
+def attention_call(kernel, operands, outs, flops, name):
+    seqs, span = operands[0].shape[:2]
+    return pl.pallas_call(
+        partial(kernel, span // row_block),
+        grid=(seqs,),
+        in_specs=[one_sequence(operand) for operand in operands],
+        out_specs=[one_sequence(out) for out in outs],
+        out_shape=outs,
+        compiler_params=pltpu.CompilerParams(vmem_limit_bytes=40 * 1024 * 1024),
+        cost_estimate=pl.CostEstimate(
+            flops=flops, bytes_accessed=16 << 20, transcendentals=seqs * span * 4 * 768
+        ),
+        name=name,
+    )(*operands)
+
+
 def middle_kernel(
     blocks, shards,
-    x_ref, o_ref, e_ref, w_out_ref, w_in_ref, w_down_ref, gains_ref,
-    mixed_ref, dx2_ref, do_ref, ffn_ref, out_ref, dgains_ref,
+    x_ref, o_ref, e_ref, w_out_ref, w_0_ref, w_1_ref, w_2_ref, w_3_ref, gains_ref,
+    mixed_ref, dx2_ref, do_ref, keep_ref, send_ref, out_ref, dgains_ref,
     act, slope, h2_all, dm_all, db_all, o_all, hid_all, dg_all, du_all,
 ):
     step = pl.program_id(0)
-    ff = w_in_ref.shape[3]
+    weights = (w_0_ref, w_1_ref, w_2_ref, w_3_ref)
+    ff = w_0_ref.shape[2]
     model = x_ref.shape[1]
     heads = out_ref.shape[2]
 
@@ -179,8 +242,8 @@
         m = jnp.zeros((row_block, model), f32)
         for s in range(shards):
             cols = slice(s * ff, (s + 1) * ff)
-            gate = dot_nn(h2, w_in_ref[s, 0])
-            up = dot_nn(h2, w_in_ref[s, 1])
+            gate = dot_nn(h2, weights[s][0])
+            up = dot_nn(h2, weights[s][1])
             c = (2.0 / jnp.pi) ** 0.5
             sq = gate * gate
             t = jnp.tanh(c * gate * (1.0 + 0.044715 * sq))
@@ -192,19 +255,19 @@
             )
             hidden = (gelu * up).astype(bf16)
             hid_all[s, rows] = hidden
-            m += dot_nn(hidden, w_down_ref[s])
+            m += dot_nt(hidden, weights[s][2])
         r_m = inverse_rms(m)
         mixed_ref[...] = (x2 + m * r_m * gain_post).astype(bf16)
         dm = rms_back(m, r_m, gain_post, e).astype(bf16)
         dh2 = jnp.zeros((row_block, model), f32)
         for s in range(shards):
             cols = slice(s * ff, (s + 1) * ff)
-            dh = dot_nt(dm, w_down_ref[s])
+            dh = dot_nn(dm, weights[s][2])
             dgate = (dh * slope[:, cols]).astype(bf16)
             dup = (dh * act[:, cols]).astype(bf16)
             dg_all[s, rows] = dgate
             du_all[s, rows] = dup
-            dh2 += dot_nt(dgate, w_in_ref[s, 0]) + dot_nt(dup, w_in_ref[s, 1])
+            dh2 += dot_nt(dgate, weights[s][0]) + dot_nt(dup, weights[s][1])
         dx2 = e + rms_back(x2, r_x2, gain_pre, dh2)
         dx2_ref[...] = dx2
         db = rms_back(branch, r_branch, gain_attn, dx2).astype(bf16)
@@ -225,18 +288,32 @@
 
     @pl.when(step >= blocks)
     def _():
-        s = step - blocks
+        turn_at = step - blocks
+        piece = lax.rem(turn_at + shards // 2, shards)
         h2_t = h2_all[...].T
-        ffn_ref[0, 0:model] = dot_nn(h2_t, dg_all[s]).astype(bf16)
-        ffn_ref[0, model : 2 * model] = dot_nn(h2_t, du_all[s]).astype(bf16)
-        ffn_ref[0, 2 * model : 3 * model] = dot_nn(dm_all[...].T, hid_all[s]).astype(bf16)
-        out_ref[0] = dot_nn(db_all[...].T, o_all[s]).astype(bf16)
-
-
-def middle(x, attended, out_grad, w_out, w_in, w_down, gains):
+        gate = dot_nn(h2_t, dg_all[piece]).astype(bf16)
+        up = dot_nn(h2_t, du_all[piece]).astype(bf16)
+        down = dot_nn(dm_all[...].T, hid_all[piece]).astype(bf16)
+        out_ref[0] = dot_nn(db_all[...].T, o_all[turn_at]).astype(bf16)
+
+        @pl.when(turn_at < shards // 2)
+        def _():
+            send_ref[0, 0:model] = gate
+            send_ref[0, model : 2 * model] = up
+            send_ref[0, 2 * model : 3 * model] = down
+
+        @pl.when(turn_at >= shards // 2)
+        def _():
+            keep_ref[0, 0:model] = gate
+            keep_ref[0, model : 2 * model] = up
+            keep_ref[0, 2 * model : 3 * model] = down
+
+
+def middle(x, attended, out_grad, w_out, weights, gains):
     rows, model = x.shape
     inner = attended.shape[1]
-    shards, _, _, ff = w_in.shape
+    shards, ff = len(weights), weights[0].shape[2]
+    half = shards // 2
     blocks = rows // row_block
     heads = inner // shards
 
@@ -246,26 +323,30 @@
     def whole(shape):
         return pl.BlockSpec(shape, lambda i: (0,) * len(shape), pipeline_mode=pl.Buffered(1))
 
-    def shard_spec(shape):
-        return pl.BlockSpec((1,) + shape, lambda i: (jnp.maximum(i - blocks, 0), 0, 0))
+    def shard_spec(shape, first, count):
+        return pl.BlockSpec(
+            (1,) + shape, lambda i: (jnp.clip(i - blocks - first, 0, count - 1), 0, 0)
+        )
 
     return pl.pallas_call(
         partial(middle_kernel, blocks, shards),
         grid=(blocks + shards,),
         in_specs=[
             row_spec(model), row_spec(inner), row_spec(model),
-            whole(w_out.shape), whole(w_in.shape), whole(w_down.shape), whole(gains.shape),
+            whole(w_out.shape), *[whole(weight.shape) for weight in weights], whole(gains.shape),
         ],
         out_specs=[
             row_spec(model), row_spec(model), row_spec(inner),
-            shard_spec((3 * model, ff)), shard_spec((model, heads)),
+            shard_spec((3 * model, ff), half, half), shard_spec((3 * model, ff), 0, half),
+            shard_spec((model, heads), 0, shards),
             pl.BlockSpec((8, model), lambda i: (0, 0)),
         ],
         out_shape=[
             jax.ShapeDtypeStruct((rows, model), bf16),
             jax.ShapeDtypeStruct((rows, model), f32),
             jax.ShapeDtypeStruct((rows, inner), bf16),
-            jax.ShapeDtypeStruct((shards, 3 * model, ff), bf16),
+            jax.ShapeDtypeStruct((half, 3 * model, ff), bf16),
+            jax.ShapeDtypeStruct((half, 3 * model, ff), bf16),
             jax.ShapeDtypeStruct((shards, model, heads), bf16),
             jax.ShapeDtypeStruct((8, model), f32),
         ],
@@ -286,7 +367,7 @@
             bytes_accessed=30 << 20, transcendentals=rows * shards * ff,
         ),
         name="middle",
-    )(x, attended, out_grad, w_out, w_in, w_down, gains)
+    )(x, attended, out_grad, w_out, *weights, gains)
 
 
 def turn_kernel(ffn_ref, attn_ref, down_ref, out_ref):
@@ -303,13 +384,6 @@
         compiler_params=pltpu.CompilerParams(vmem_limit_bytes=24 * 1024 * 1024),
         name="turn",
     )(ffn_part, attn_part)
-
-
-def score_block(queries, key_rows, allowed):
-    scores = jnp.einsum(
-        "sqhd,skd->shqk", queries, key_rows, preferred_element_type=jnp.float32
-    ) * HEAD ** (-0.5)
-    return jnp.where(allowed[:, None], scores, masked_score)
 
 
 def adam_step(weight, gradient, moment, square, step_rate, decay_rate):
@@ -346,11 +420,9 @@
 ):
     seqs_here, span_rows, model_width = block_input.shape
     row_count = seqs_here * span_rows
-    w_qkv, w_out, w_ffin, w_ffout, gains_low = (
+    w_qkv, w_out, gains_low = (
         lax.all_gather(qkv_weight.astype(jnp.bfloat16), "shard", axis=1, tiled=True),
         lax.all_gather(out_weight.astype(jnp.bfloat16), "shard", axis=0, tiled=True),
-        lax.all_gather(ff_in_weight.astype(jnp.bfloat16), "shard", axis=0),
-        lax.all_gather(ff_out_weight.astype(jnp.bfloat16), "shard", axis=0),
         lax.all_gather(norm_gains.astype(jnp.bfloat16), "shard", axis=0, tiled=True),
     )
     gain_in, gain_attn, gain_pre, gain_post, gain_query, gain_key = split_gains(
@@ -358,78 +430,66 @@
     )
     tokens = block_input.astype(jnp.float32).reshape(row_count, model_width)
     normed = rms_scale(tokens, gain_in).astype(jnp.bfloat16)
+    ffn_own = jnp.concatenate(
+        [ff_in_weight.astype(jnp.bfloat16), ff_out_weight.astype(jnp.bfloat16).T[None]], axis=0
+    )
+    ffn_own, w_qkv = together(ffn_own, w_qkv)
+    ffn_x = swap_bit(ffn_own, "shard", 1)
+    ffn_core = swap_bit(ffn_own, "shard", 0)
+    ffn_both = swap_bit(ffn_x, "shard", 0)
     project = jnp.dot(normed, w_qkv, preferred_element_type=jnp.float32).reshape(
         seqs_here, span_rows, -1
     )
+    pieces = [project[..., i * HEAD : (i + 1) * HEAD] for i in range(QH + 2)]
     cos_table, sine_table = rope_tables(positions)
     query_full, key_full, value_full = head_post(
-        project, gain_query, gain_key, cos_table, sine_table
-    )
-    queries = query_full.astype(jnp.bfloat16)
+        pieces, gain_query, gain_key, cos_table, sine_table
+    )
+    queries = jnp.concatenate([part.astype(jnp.bfloat16) for part in query_full], axis=-1)
     keys_own = key_full.astype(jnp.bfloat16)
     values_own = value_full.astype(jnp.bfloat16)
     key_prev, value_prev, segment_prev = from_behind((keys_own, values_own, segments), "seq", 1)
     is_first = lax.axis_index("seq") == 0
-    distance = jnp.arange(span_rows)[:, None] - (jnp.arange(WINDOW + span_rows)[None, :] - WINDOW)
-    in_window = (distance >= 0) & (distance < WINDOW)
-    from_prev = (jnp.arange(WINDOW + span_rows) >= WINDOW) | jnp.logical_not(is_first)
-    key_segments = jnp.concatenate([segment_prev, segments], axis=1)
-    same_doc = segments[:, :, None] == key_segments[:, None, :]
-    allowed = in_window[None] & from_prev[None, None, :] & same_doc
+    key_segments = jnp.concatenate([jnp.where(is_first, -1, segment_prev), segments], axis=1)
     all_keys = jnp.concatenate([key_prev, keys_own], axis=1)
     all_values = jnp.concatenate([value_prev, values_own], axis=1)
-    scores = score_block(queries, all_keys, allowed)
-    row_top = jnp.max(scores, axis=-1, keepdims=True)
-    exp_terms = jnp.exp(scores - row_top)
-    row_total = jnp.sum(exp_terms, axis=-1, keepdims=True)
-    attn_probs = exp_terms / row_total
-    log_total = row_top + jnp.log(row_total)
-    attended = jnp.einsum(
-        "shqk,skd->sqhd",
-        attn_probs.astype(jnp.bfloat16),
-        all_values,
-        preferred_element_type=jnp.float32,
-    )
-    attended_low = attended.reshape(row_count, QH * HEAD).astype(jnp.bfloat16)
+    operands = (queries, all_keys, all_values, segments[:, :, None], key_segments[:, None, :])
+    attention_flops = 2 * 2 * row_count * QH * (WINDOW + row_block) * HEAD
+    (attended_low,) = attention_call(
+        attend_kernel,
+        operands,
+        [jax.ShapeDtypeStruct(queries.shape, jnp.bfloat16)],
+        attention_flops,
+        "attend",
+    )
+    attended_low = attended_low.reshape(row_count, QH * HEAD)
     shards = lax.axis_size("shard")
     low_dot = partial(jnp.einsum, preferred_element_type=jnp.float32)
-    mixed, grad_middle, grad_attended, ffn_parts, out_parts, grad_three = middle(
+    mixed, grad_middle, grad_attended, ffn_keep, ffn_send, out_parts, grad_three = middle(
         block_input.reshape(row_count, model_width),
         attended_low,
         out_grad.reshape(row_count, model_width),
         w_out,
-        w_ffin,
-        w_ffout,
+        (ffn_own, ffn_x, ffn_core, ffn_both),
         jnp.stack([gain_attn, gain_pre, gain_post]),
     )
     mixed = mixed.reshape(block_input.shape)
     grad_gain_attn, grad_gain_pre, grad_gain_post = grad_three[0], grad_three[1], grad_three[2]
-    grad_attended = grad_attended.reshape(seqs_here, span_rows, QH, HEAD)
-    ffn_steps = reduce_steps(ffn_parts)
-    ffn_sum = next(ffn_steps)
-    scores_back = score_block(queries, all_keys, allowed)
-    scores_back, ffn_sum = together(scores_back, ffn_sum)
-    ffn_sum = advance(ffn_steps, ffn_sum)
-    probs_back = jnp.exp(scores_back - log_total)
-    grad_values = jnp.einsum(
-        "shqk,sqhd->skd",
-        probs_back.astype(jnp.bfloat16),
-        grad_attended,
-        preferred_element_type=jnp.float32,
-    )
-    grad_probs = jnp.einsum(
-        "sqhd,skd->shqk", grad_attended, all_values, preferred_element_type=jnp.float32
-    )
-    inner_sum = jnp.sum(probs_back * grad_probs, axis=-1, keepdims=True)
-    grad_scores = (probs_back * (grad_probs - inner_sum)).astype(jnp.bfloat16)
-    grad_scores, ffn_sum = together(grad_scores, ffn_sum)
-    ffn_sum = advance(ffn_steps, ffn_sum)
-    grad_queries = jnp.einsum(
-        "shqk,skd->sqhd", grad_scores, all_keys, preferred_element_type=jnp.float32
-    ) * HEAD ** (-0.5)
-    grad_keys = jnp.einsum(
-        "shqk,sqhd->skd", grad_scores, queries, preferred_element_type=jnp.float32
-    ) * HEAD ** (-0.5)
+    ffn_came = swap_bit(ffn_send, "shard", 0)
+    grad_queries, grad_keys, grad_values = attention_call(
+        attend_back_kernel,
+        operands + (grad_attended.reshape(queries.shape),),
+        [
+            jax.ShapeDtypeStruct(queries.shape, jnp.float32),
+            jax.ShapeDtypeStruct(all_keys.shape, jnp.float32),
+            jax.ShapeDtypeStruct(all_keys.shape, jnp.float32),
+        ],
+        attention_flops * 5 // 2,
+        "attend_back",
+    )
+    grad_queries, ffn_came = together(grad_queries, ffn_came)
+    ffn_pair = ffn_keep.astype(jnp.float32) + ffn_came.astype(jnp.float32)
+    ffn_came = swap_bit(ffn_pair[1].astype(jnp.bfloat16), "shard", 1)
     grad_key_next, grad_value_next = (
         from_behind(grad_keys[:, :WINDOW].astype(jnp.bfloat16), "seq", -1).astype(jnp.float32),
         from_behind(grad_values[:, :WINDOW].astype(jnp.bfloat16), "seq", -1).astype(jnp.float32),
@@ -438,16 +498,23 @@
     grad_value_own = grad_values[:, WINDOW:] + grad_value_next
     head_back = jax.vjp(
         partial(head_post, cos_table=cos_table, sine_table=sine_table),
-        project,
+        pieces,
         gain_query,
         gain_key,
     )[1]
-    grad_project, grad_gain_query, grad_gain_key = head_back(
-        (grad_queries, grad_key_own, grad_value_own)
-    )
-    grad_project_low = grad_project.reshape(row_count, -1).astype(jnp.bfloat16)
-    grad_project_low, ffn_sum = together(grad_project_low, ffn_sum)
-    ffn_sum = advance(ffn_steps, ffn_sum)
+    grad_pieces, grad_gain_query, grad_gain_key = head_back(
+        (
+            [grad_queries[..., i * HEAD : (i + 1) * HEAD] for i in range(QH)],
+            grad_key_own,
+            grad_value_own,
+        )
+    )
+    grad_project_low = jnp.concatenate(
+        [piece.astype(jnp.bfloat16) for piece in grad_pieces], axis=-1
+    ).reshape(row_count, -1)
+    grad_project_low, ffn_came = together(grad_project_low, ffn_came)
+    ffn_steps = seq_steps((ffn_pair[0] + ffn_came.astype(jnp.float32)).astype(jnp.bfloat16))
+    ffn_sum = next(ffn_steps)
     grad_normed = jnp.einsum(
         "nk,dk->nd", grad_project_low, w_qkv, preferred_element_type=jnp.float32
     )

time: 427 us -> 426 us (level)
  waiting for transfers between devices: 126 us -> 183 us
  matrix products: 54.2 us -> 10.8 us
  Pallas kernels: 52 us -> 77.2 us
  other arithmetic: 95.3 us -> 72.9 us
  local copies, waits for them, and re-layouts: 35.9 us -> 19.6 us
    ppermute x16 -> x19, waiting for transfers between devices: 84.3 us -> 156 us  [swap_bit(): lax.ppermute(block, axis, [(i, i ^ 1 << bit) for i in range(lax.axis_size...]
    dot_general x6 -> x0, matrix products: 43.3 us -> none  [the longest x1 10.4 us: on_device(): jnp.einsum('shqk,skd->sqhd', attn_probs.astype(jnp.bfloat16), all_values,...]
    all_gather x2 -> x0, waiting for transfers between devices: 25.3 us -> none  [the longest x1 25.3 us: on_device(): lax.all_gather(ff_in_weight.astype(jnp.bfloat16), 'shard', axis=0)]
    pallas_call x0 -> x2, Pallas kernels: none -> 24.4 us  [attention_call(): pl.pallas_call(partial(kernel, span // row_block), grid=(seqs,), in_specs...]
    sub x2 -> x0, other arithmetic: 22.6 us -> none  [the longest x1 22.6 us: on_device(): grad_scores = (probs_back * (grad_probs - inner_sum)).astype(jnp.bfloat16)]
    unnamed x3 -> x15, other arithmetic: 1.89 us -> 18.8 us
    reshape x3 -> x0, local copies, waits for them, and re-layouts: 9.82 us -> none  [the longest x2 6.24 us: head_post(): queries = project[..., :QH * HEAD].reshape(project.shape[:-1] + (QH, HEAD))]
    ppermute x5, waiting for transfers between devices: 12 us -> 20.7 us  [from_behind(): return lax.ppermute(block, axis, route)]
  transfers between devices with their start and end apart: 25 -> 26, of which waited for: 16 -> 15; matrix products, arithmetic and copies ran while one was open for 33% -> 17% of each run, Pallas kernels for 0% -> 6%
where the time goes in v3:
time: 426 us; the launch traced here: 419 us
  waiting for transfers between devices  183 us (43%)
  Pallas kernels  77.2 us (18%)
  other arithmetic  72.9 us (17%)
  starting transfers between devices  34.3 us (8%)
  local copies, waits for them, and re-layouts  19.6 us (5%)
  between operations  15.7 us (4%)
  matrix products  10.8 us (3%)
  blocking collectives  5.16 us (1%)
    ppermute x19, waiting for transfers between devices, swap_bit(): lax.ppermute(block, axis, [(i, i ^ 1 << bit) for i in range(lax.axis_size...  156 us
    pallas_call x1, Pallas kernels, middle(): pl.pallas_call(partial(middle_kernel, blocks, shards), grid=(blocks + sha...  52.5 us
    pallas_call x2, Pallas kernels, attention_call(): pl.pallas_call(partial(kernel, span // row_block), grid=(seqs,), in_specs...  24.4 us
    ppermute x5, waiting for transfers between devices, from_behind(): return lax.ppermute(block, axis, route)  20.7 us
    ppermute x19, starting transfers between devices, swap_bit(): lax.ppermute(block, axis, [(i, i ^ 1 << bit) for i in range(lax.axis_size...  19.2 us
    unnamed x15, other arithmetic  18.8 us
    ppermute x5, starting transfers between devices, from_behind(): return lax.ppermute(block, axis, route)  15 us
    unnamed x102, local copies, waits for them, and re-layouts  14.1 us
  transfers between devices with their start and end apart: 26, of which 15 were waited for; matrix products, arithmetic and copies ran while one was open for 17% of the time, Pallas kernels for 6%

profile of v3, /device:TPU:0, one launch (start us, length us, event | category | flops | bytes accessed | tf_op | source)
XLA Modules:
  0.0 419.0 jit_solution(15961066546300729172)
XLA Ops:
  9.5 4.9 %collective-permute-start.2 = (s32[2,512]{1,0:T(2,128)}, s32[2,512]{1,0:T(2,128)S(1)}, u32[]{:S(2)}, u32[]{:S(2)}) collective-permute-start(s32[2,512]{1,0:T(2,128)} %param.22), channel_id=1, source_target_pairs={{0,4},{4,8},{8,12},{12,16},{16,20},{20,24},{24,28},{1,5},{5,9},{9,... | collective-permute-start | bytes 12296 | tf_op jit(solution)/shard_map/ppermute | solution.py:31
  15.3 5.2 %all-gather = bf16[4,1,768]{2,1,0:T(2,128)(2,1)S(1)} all-gather(bf16[1,1,768]{2,1,0:T(2,128)(2,1)S(1)} %reshape.278), channel_id=1, replica_groups=mesh['seq'=8,'shard'=4] {'shard'}, dimensions={0}, use_global_device_ids=true | all-gather | bytes 7680 | tf_op jit(solution)/shard_map/all_gather | solution.py:426
  28.1 6.6 %all-gather.4.cloned.1.call-done = bf16[640,1536]{1,0:T(8,128)(2,1)} async-done(((bf16[640,384]{1,0:T(8,128)(2,1)}), bf16[640,1536]{1,0:T(8,128)(2,1)}) %all-gather.4.cloned.1.call-update) | async-done | bytes 1966096 | tf_op jit(solution)/shard_map/all_gather | solution.py:424
  35.1 4.2 %fusion.19 = f32[2,512,1536]{2,1,0:T(8,128)S(1)} fusion(bf16[640,1536]{1,0:T(8,128)(2,1)} %all-gather.4.cloned.1.call-done, bf16[2,512,640]{2,1,0:T(8,128)(2,1)S(1)} %copy-done.16, f32[640]{0:T(1024)S(1)} %get-tuple-element.129, f32[2,512]{1,0:T(2,128)S(1)} %get-tuple-element.133), kind=kOutput, calls=%fused_computation.38 | convolution fusion | flops 2015887360 | bytes 9574912 | tf_op jit(solution)/shard_map/dot_general | solution.py:440
  43.4 3.6 collective-permute-start
  51.8 35.2 %collective-permute-done.3.w_1_ref = bf16[3,640,512]{2,1,0:T(8,128)(2,1)} collective-permute-done((bf16[3,640,512]{2,1,0:T(8,128)(2,1)}, bf16[3,640,512]{2,1,0:T(8,128)(2,1)}, u32[]{:S(2)}, u32[]{:S(2)}) %collective-permute-start.3) | collective-permute-done | bytes 1966112 | tf_op jit(solution)/shard_map/ppermute | solution.py:35
  97.0 3.9 collective-permute-start.1
  106.0 6.3 %collective-permute-done.1 = bf16[2,512,256]{2,1,0:T(8,128)(2,1)S(1)} collective-permute-done((bf16[2,512,256]{2,1,0:T(8,128)(2,1)S(1)}, bf16[2,512,256]{2,1,0:T(8,128)(2,1)S(1)}, u32[]{:S(2)}, u32[]{:S(2)}) %collective-permute-start.1) | collective-permute-done | bytes 524320 | tf_op jit(solution)/shard_map/ppermute | solution.py:31
  112.4 7.5 %attend.1 = bf16[2,512,1024]{2,1,0:T(8,128)(2,1)S(1)} custom-call(bf16[2,512,1024]{2,1,0:T(8,128)(2,1)S(1)} %fusion.114.q_ref, bf16[2,1024,256]{2,1,0:T(8,128)(2,1)S(1)} %maximum_maximum_fusion.k_ref, bf16[2,1024,256]{2,1,0:T(8,128)(2,1)S(1)} %pad_maximum_fusion.2.v_ref, s32[2,512,1]{2,1,0:T(8,128)S(1)} %copy.48.seg_q_ref, ...), custom_call_target="tpu_custom_call" | custom-call | flops 3221225472 | bytes 16777216 | tf_op jit(solution)/shard_map/attend/pallas_call | solution.py:204
  122.2 52.5 %middle.1 = (bf16[1024,640]{1,0:T(8,128)(2,1)}, f32[1024,640]{1,0:T(8,128)}, bf16[1024,1024]{1,0:T(8,128)(2,1)}, bf16[2,1920,512]{2,1,0:T(8,128)(2,1)}, bf16[2,1...) custom-call(bf16[1024,640]{1,0:T(8,128)(2,1)} %bitcast.118, bf16[1024,1024]{1,0:T(8,128)(2,1)} %bitcast.109, ...), custom_call_target="tpu_custom_call" | custom-call | flops 28185722880 | bytes 31457280 | tf_op jit(solution)/shard_map/middle/pallas_call | solution.py:331
  176.4 16.9 %attend_back.1 = (f32[2,512,1024]{2,1,0:T(8,128)}, f32[2,1024,256]{2,1,0:T(8,128)S(1)}, f32[2,1024,256]{2,1,0:T(8,128)S(1)}) custom-call(bf16[2,512,1024]{2,1,0:T(8,128)(2,1)S(1)} %copy-done.6, bf16[2,1024,256]{2,1,0:T(8,128)(2,1)S(1)} %maximum_maximum_fusion.k_ref, bf16[2,1024,256]{2,1,0:T(8,128)(2,1)S(1)} %copy-done.2, s32[2,512,1]{2,1,0:T(8,128)S(1)} %copy-done.4, ...), custom_call_target="tpu_custom_call" | custom-call | flops 8053063680 | bytes 16777216 | tf_op jit(solution)/shard_map/attend_back/pallas_call | solution.py:204
  197.4 14.4 %collective-permute-done.7 = bf16[2,512,256]{2,1,0:T(8,128)(2,1)S(1)} collective-permute-done((bf16[2,512,256]{2,1,0:T(8,128)(2,1)S(1)}, bf16[2,512,256]{2,1,0:T(8,128)(2,1)S(1)}, u32[]{:S(2)}, u32[]{:S(2)}) %collective-permute-start.7) | collective-permute-done | bytes 524320 | tf_op jit(solution)/shard_map/ppermute | solution.py:31
  229.9 35.5 %collective-permute-done.9 = bf16[1920,512]{1,0:T(8,128)(2,1)S(1)} collective-permute-done((bf16[1920,512]{1,0:T(8,128)(2,1)S(1)}, bf16[1920,512]{1,0:T(8,128)(2,1)S(1)}, u32[]{:S(2)}, u32[]{:S(2)}) %collective-permute-start.9) | collective-permute-done | bytes 1966112 | tf_op jit(solution)/shard_map/ppermute | solution.py:35
  265.4 4.3 %fusion.12 = (bf16[640]{0:T(1024)(128)(2,1)S(1)}, f32[1024]{0:T(1024)S(1)}, bf16[1024,640]{1,0:T(8,128)(2,1)S(1)}, f32[1024,640]{1,0:T(8,128)}) fusion(bf16[2,512,640]{2,1,0:T(8,128)(2,1)S(1)} %copy-done.17, f32[1024]{0:T(1024)S(1)} %rsqrt.75, f32[640]{0:T(1024)S(1)} %get-tuple-element.129, bf16[1024,1536]{1,0:T(8,128)(2,1)S(1)} %bitcast.132, ...), kind=kOutput, calls=%fused_computation.27 | convolution fusion | flops 2019162496 | bytes 10366720 | tf_op jit(solution)/shard_map/nk,dk->nd/dot_general | solution.py:518
  284.7 22.7 %collective-permute-done.18 = bf16[960,512]{1,0:T(8,128)(2,1)} collective-permute-done((bf16[960,512]{1,0:T(8,128)(2,1)}, bf16[960,512]{1,0:T(8,128)(2,1)}, u32[]{:S(2)}, u32[]{:S(2)}) %collective-permute-start.18) | collective-permute-done | bytes 983072 | tf_op jit(solution)/shard_map/ppermute | solution.py:35
  315.1 8.1 %collective-permute-done.19 = bf16[480,512]{1,0:T(8,128)(2,1)} collective-permute-done((bf16[480,512]{1,0:T(8,128)(2,1)}, bf16[480,512]{1,0:T(8,128)(2,1)}, u32[]{:S(2)}, u32[]{:S(2)}) %collective-permute-start.19) | collective-permute-done | bytes 491552 | tf_op jit(solution)/shard_map/ppermute | solution.py:35
  327.9 10.7 %collective-permute-done.20 = bf16[240,512]{1,0:T(8,128)(2,1)} collective-permute-done((bf16[240,512]{1,0:T(8,128)(2,1)S(1)}, bf16[240,512]{1,0:T(8,128)(2,1)}, u32[]{:S(2)}, u32[]{:S(2)}) %collective-permute-start.20) | collective-permute-done | bytes 245792 | tf_op jit(solution)/shard_map/ppermute | solution.py:35
  342.6 10.4 %collective-permute-done.21 = bf16[240,512]{1,0:T(8,128)(2,1)S(1)} collective-permute-done((bf16[240,512]{1,0:T(8,128)(2,1)S(1)}, bf16[240,512]{1,0:T(8,128)(2,1)S(1)}, u32[]{:S(2)}, u32[]{:S(2)}) %collective-permute-start.21) | collective-permute-done | bytes 245792 | tf_op jit(solution)/shard_map/ppermute | solution.py:35
  353.4 3.8 collective-permute-start.13
  357.3 10.1 %collective-permute-done.22 = bf16[480,512]{1,0:T(8,128)(2,1)S(1)} collective-permute-done((bf16[480,512]{1,0:T(8,128)(2,1)S(1)}, bf16[480,512]{1,0:T(8,128)(2,1)S(1)}, u32[]{:S(2)}, u32[]{:S(2)}) %collective-permute-start.22) | collective-permute-done | bytes 491552 | tf_op jit(solution)/shard_map/ppermute | solution.py:35
  373.1 3.4 collective-permute-done.14
  377.1 11.6 %collective-permute-done.23 = bf16[960,512]{1,0:T(8,128)(2,1)S(1)} collective-permute-done((bf16[960,512]{1,0:T(8,128)(2,1)S(1)}, bf16[960,512]{1,0:T(8,128)(2,1)S(1)}, u32[]{:S(2)}, u32[]{:S(2)}) %collective-permute-start.23) | collective-permute-done | bytes 983072 | tf_op jit(solution)/shard_map/ppermute | solution.py:35
  390.0 5.3 %collective-permute-done.16 = bf16[176,640]{1,0:T(8,128)(2,1)S(1)} collective-permute-done((bf16[176,640]{1,0:T(8,128)(2,1)S(1)}, bf16[176,640]{1,0:T(8,128)(2,1)S(1)}, u32[]{:S(2)}, u32[]{:S(2)}) %collective-permute-start.16) | collective-permute-done | bytes 225312 | tf_op jit(solution)/shard_map/ppermute | solution.py:35
  397.2 4.7 %multiply_subtract_fusion = (f32[2,640,512]{2,1,0:T(8,128)}, f32[2,640,512]{2,1,0:T(8,128)}, f32[2,640,512]{2,1,0:T(8,128)}) fusion(f32[2,640,512]{2,1,0:T(8,128)S(1)} %copy-done.14, bf16[2,640,512]{2,1,0:T(8,128)(2,1)S(1)} %bitcast.117, f32[2,640,512]{2,1,0:T(8,128)S(1)} %copy-done.27, f32[2,640,512]{2,1,0:T(8,128)S(1)} %copy-done.28), kind=kLoop, calls=%fused_computation.32 | loop fusion | flops 10485760 | bytes 17039360 | tf_op jit(solution)/shard_map/sub | solution.py:394
  (246 shorter events, 111.5 us)
Async XLA Ops:
  7.2 27.5 %all-gather.4.cloned.1.call-start = ((), (), s32[]{:S(2)}) async-start(), calls=%async_computation | async-start | bytes 2457600 | tf_op jit(solution)/shard_map/all_gather | solution.py:424
  9.5 112.7 %all-gather.6.cloned.1.call-start = ((), (), s32[]{:S(2)}) async-start(), calls=%async_computation.1 | async-start | bytes 1638400 | tf_op jit(solution)/shard_map/all_gather | solution.py:425
  9.5 18.5 %collective-permute-start.2 = (s32[2,512]{1,0:T(2,128)}, s32[2,512]{1,0:T(2,128)S(1)}, u32[]{:S(2)}, u32[]{:S(2)}) collective-permute-start(s32[2,512]{1,0:T(2,128)} %param.22), channel_id=1, source_target_pairs={{0,4},{4,8},{8,12},{12,16},{16,20},{20,24},{24,28},{1,5},{5,9},{9,... | collective-permute-start | bytes 12296 | tf_op jit(solution)/shard_map/ppermute | solution.py:31
  34.8 52.3 %collective-permute-start.3 = (bf16[3,640,512]{2,1,0:T(8,128)(2,1)}, bf16[3,640,512]{2,1,0:T(8,128)(2,1)}, u32[]{:S(2)}, u32[]{:S(2)}) collective-permute-start(bf16[3,640,512]{2,1,0:T(8,128)(2,1)} %pad_maximum_fusion.w_0_ref), channel_id=1, source_target_pairs={{0,2},{1,3},{2,0},{3,1},{4,6},{5,7},{6,4},{7,5},{8,10},{9,11},{10,... | collective-permute-start | bytes 5898248 | tf_op jit(solution)/shard_map/ppermute | solution.py:35
  35.1 87.1 %collective-permute-start.4 = (bf16[3,640,512]{2,1,0:T(8,128)(2,1)}, bf16[3,640,512]{2,1,0:T(8,128)(2,1)}, u32[]{:S(2)}, u32[]{:S(2)}) collective-permute-start(bf16[3,640,512]{2,1,0:T(8,128)(2,1)} %pad_maximum_fusion.w_0_ref), channel_id=1, source_target_pairs={{0,1},{1,0},{2,3},{3,2},{4,5},{5,4},{6,7},{7,6},{8,9},{9,8},{10,11... | collective-permute-start | bytes 5898248 | tf_op jit(solution)/shard_map/ppermute | solution.py:35
  43.4 62.5 %collective-permute-start = (bf16[2,512,256]{2,1,0:T(8,128)(2,1)S(1)}, bf16[2,512,256]{2,1,0:T(8,128)(2,1)S(1)}, u32[]{:S(2)}, u32[]{:S(2)}) collective-permute-start(bf16[2,512,256]{2,1,0:T(8,128)(2,1)S(1)} %pad_maximum_fusion.4), channel_id=1, source_target_pairs={{0,4},{4,8},{8,12},{12,16},{16,20},{20,24},{24,28},{1,5},{5,9},{9,... | collective-permute-start | bytes 1572872 | tf_op jit(solution)/shard_map/ppermute | solution.py:31
  87.1 35.1 %collective-permute-start.5 = (bf16[3,640,512]{2,1,0:T(8,128)(2,1)}, bf16[3,640,512]{2,1,0:T(8,128)(2,1)}, u32[]{:S(2)}, u32[]{:S(2)}) collective-permute-start(bf16[3,640,512]{2,1,0:T(8,128)(2,1)} %collective-permute-done.3.w_1_ref), channel_id=1, source_target_pairs={{0,1},{1,0},{2,3},{3,2},{4,5},{5,4},{6,7},{7,6},{8,9},{9,8},{10,11... | collective-permute-start | bytes 5898248 | tf_op jit(solution)/shard_map/ppermute | solution.py:35
  97.0 15.2 %collective-permute-start.1 = (bf16[2,512,256]{2,1,0:T(8,128)(2,1)S(1)}, bf16[2,512,256]{2,1,0:T(8,128)(2,1)S(1)}, u32[]{:S(2)}, u32[]{:S(2)}) collective-permute-start(bf16[2,512,256]{2,1,0:T(8,128)(2,1)S(1)} %slice.322), channel_id=1, source_target_pairs={{0,4},{4,8},{8,12},{12,16},{16,20},{20,24},{24,28},{1,5},{5,9},{9,... | collective-permute-start | bytes 1572872 | tf_op jit(solution)/shard_map/ppermute | solution.py:31
  174.7 42.4 %collective-permute-start.6 = (bf16[2,1920,512]{2,1,0:T(8,128)(2,1)}, bf16[2,1920,512]{2,1,0:T(8,128)(2,1)}, u32[]{:S(2)}, u32[]{:S(2)}) collective-permute-start(bf16[2,1920,512]{2,1,0:T(8,128)(2,1)} %get-tuple-element.41), channel_id=1, source_target_pairs={{0,1},{1,0},{2,3},{3,2},{4,5},{5,4},{6,7},{7,6},{8,9},{9,8},{10,11... | collective-permute-start | bytes 11796488 | tf_op jit(solution)/shard_map/ppermute | solution.py:35
  194.7 17.2 %collective-permute-start.7 = (bf16[2,512,256]{2,1,0:T(8,128)(2,1)S(1)}, bf16[2,512,256]{2,1,0:T(8,128)(2,1)S(1)}, u32[]{:S(2)}, u32[]{:S(2)}) collective-permute-start(bf16[2,512,256]{2,1,0:T(8,128)(2,1)S(1)} %slice.321), channel_id=1, source_target_pairs={{4,0},{8,4},{12,8},{16,12},{20,16},{24,20},{28,24},{5,1},{9,5},{13... | collective-permute-start | bytes 1572872 | tf_op jit(solution)/shard_map/ppermute | solution.py:31
  196.1 33.6 %collective-permute-start.8 = (bf16[2,512,256]{2,1,0:T(8,128)(2,1)S(1)}, bf16[2,512,256]{2,1,0:T(8,128)(2,1)S(1)}, u32[]{:S(2)}, u32[]{:S(2)}) collective-permute-start(bf16[2,512,256]{2,1,0:T(8,128)(2,1)S(1)} %slice.320), channel_id=1, source_target_pairs={{4,0},{8,4},{12,8},{16,12},{20,16},{24,20},{28,24},{5,1},{9,5},{13... | collective-permute-start | bytes 1572872 | tf_op jit(solution)/shard_map/ppermute | solution.py:31
  220.9 44.5 %collective-permute-start.9 = (bf16[1920,512]{1,0:T(8,128)(2,1)S(1)}, bf16[1920,512]{1,0:T(8,128)(2,1)S(1)}, u32[]{:S(2)}, u32[]{:S(2)}) collective-permute-start(bf16[1920,512]{1,0:T(8,128)(2,1)S(1)} %fusion.17), channel_id=1, source_target_pairs={{0,2},{1,3},{2,0},{3,1},{4,6},{5,7},{6,4},{7,5},{8,10},{9,11},{10,... | collective-permute-start | bytes 5898248 | tf_op jit(solution)/shard_map/ppermute | solution.py:35
  278.4 33.2 %collective-permute-start.10 = (bf16[2,704,640]{2,1,0:T(8,128)(2,1)}, bf16[2,704,640]{2,1,0:T(8,128)(2,1)}, u32[]{:S(2)}, u32[]{:S(2)}) collective-permute-start(bf16[2,704,640]{2,1,0:T(8,128)(2,1)} %dynamic-slice_bitcast_fusion), channel_id=1, source_target_pairs={{0,1},{1,0},{2,3},{3,2},{4,5},{5,4},{6,7},{7,6},{8,9},{9,8},{10,11... | collective-permute-start | bytes 5406728 | tf_op jit(solution)/shard_map/ppermute | solution.py:35
  282.3 25.2 %collective-permute-start.18 = (bf16[960,512]{1,0:T(8,128)(2,1)}, bf16[960,512]{1,0:T(8,128)(2,1)}, u32[]{:S(2)}, u32[]{:S(2)}) collective-permute-start(bf16[960,512]{1,0:T(8,128)(2,1)} %dynamic-slice_bitcast_fusion.1), channel_id=1, source_target_pairs={{0,4},{4,0},{8,12},{12,8},{16,20},{20,16},{24,28},{28,24},{1,5},{5... | collective-permute-start | bytes 2949128 | tf_op jit(solution)/shard_map/ppermute | solution.py:35
  309.9 13.4 %collective-permute-start.19 = (bf16[480,512]{1,0:T(8,128)(2,1)}, bf16[480,512]{1,0:T(8,128)(2,1)}, u32[]{:S(2)}, u32[]{:S(2)}) collective-permute-start(bf16[480,512]{1,0:T(8,128)(2,1)} %dynamic-slice_bitcast_fusion.2), channel_id=1, source_target_pairs={{0,8},{4,12},{8,0},{12,4},{16,24},{20,28},{24,16},{28,20},{1,9},{5... | collective-permute-start | bytes 1474568 | tf_op jit(solution)/shard_map/ppermute | solution.py:35
  314.6 25.2 %collective-permute-start.11 = (bf16[1,704,640]{2,1,0:T(8,128)(2,1)}, bf16[1,704,640]{2,1,0:T(8,128)(2,1)}, u32[]{:S(2)}, u32[]{:S(2)}) collective-permute-start(bf16[1,704,640]{2,1,0:T(8,128)(2,1)} %constant_dynamic-slice_fusion), channel_id=1, source_target_pairs={{0,2},{1,3},{2,0},{3,1},{4,6},{5,7},{6,4},{7,5},{8,10},{9,11},{10,... | collective-permute-start | bytes 2703368 | tf_op jit(solution)/shard_map/ppermute | solution.py:35
  325.3 13.3 %collective-permute-start.20 = (bf16[240,512]{1,0:T(8,128)(2,1)S(1)}, bf16[240,512]{1,0:T(8,128)(2,1)}, u32[]{:S(2)}, u32[]{:S(2)}) collective-permute-start(bf16[240,512]{1,0:T(8,128)(2,1)S(1)} %dynamic-slice_bitcast_fusion.4), channel_id=1, source_target_pairs={{0,16},{4,20},{8,24},{12,28},{16,0},{20,4},{24,8},{28,12},{1,17},{... | collective-permute-start | bytes 737288 | tf_op jit(solution)/shard_map/ppermute | solution.py:35
  339.7 13.3 %collective-permute-start.21 = (bf16[240,512]{1,0:T(8,128)(2,1)S(1)}, bf16[240,512]{1,0:T(8,128)(2,1)S(1)}, u32[]{:S(2)}, u32[]{:S(2)}) collective-permute-start(bf16[240,512]{1,0:T(8,128)(2,1)S(1)} %fusion.112), channel_id=1, source_target_pairs={{0,16},{4,20},{8,24},{12,28},{16,0},{20,4},{24,8},{28,12},{1,17},{... | collective-permute-start | bytes 737288 | tf_op jit(solution)/shard_map/ppermute | solution.py:35
  341.3 11.9 %collective-permute-start.12 = (bf16[352,640]{1,0:T(8,128)(2,1)S(1)}, bf16[352,640]{1,0:T(8,128)(2,1)S(1)}, u32[]{:S(2)}, u32[]{:S(2)}) collective-permute-start(bf16[352,640]{1,0:T(8,128)(2,1)S(1)} %dynamic-slice_bitcast_fusion.3), channel_id=1, source_target_pairs={{0,4},{4,0},{8,12},{12,8},{16,20},{20,16},{24,28},{28,24},{1,5},{5... | collective-permute-start | bytes 1351688 | tf_op jit(solution)/shard_map/ppermute | solution.py:35
  353.1 14.2 %collective-permute-start.22 = (bf16[480,512]{1,0:T(8,128)(2,1)S(1)}, bf16[480,512]{1,0:T(8,128)(2,1)S(1)}, u32[]{:S(2)}, u32[]{:S(2)}) collective-permute-start(bf16[480,512]{1,0:T(8,128)(2,1)S(1)} %pad_maximum_fusion.5), channel_id=1, source_target_pairs={{0,8},{4,12},{8,0},{12,4},{16,24},{20,28},{24,16},{28,20},{1,9},{5... | collective-permute-start | bytes 1474568 | tf_op jit(solution)/shard_map/ppermute | solution.py:35
  353.4 16.3 %collective-permute-start.13 = (bf16[176,640]{1,0:T(8,128)(2,1)S(1)}, bf16[176,640]{1,0:T(8,128)(2,1)S(1)}, u32[]{:S(2)}, u32[]{:S(2)}) collective-permute-start(bf16[176,640]{1,0:T(8,128)(2,1)S(1)} %dynamic-slice_bitcast_fusion.5), channel_id=1, source_target_pairs={{0,8},{4,12},{8,0},{12,4},{16,24},{20,28},{24,16},{28,20},{1,9},{5... | collective-permute-start | bytes 675848 | tf_op jit(solution)/shard_map/ppermute | solution.py:35
  367.6 21.1 %collective-permute-start.23 = (bf16[960,512]{1,0:T(8,128)(2,1)S(1)}, bf16[960,512]{1,0:T(8,128)(2,1)S(1)}, u32[]{:S(2)}, u32[]{:S(2)}) collective-permute-start(bf16[960,512]{1,0:T(8,128)(2,1)S(1)} %pad_maximum_fusion.3), channel_id=1, source_target_pairs={{0,4},{4,0},{8,12},{12,8},{16,20},{20,16},{24,28},{28,24},{1,5},{5... | collective-permute-start | bytes 2949128 | tf_op jit(solution)/shard_map/ppermute | solution.py:35
  376.6 12.6 %collective-permute-start.15 = (bf16[88,640]{1,0:T(8,128)(2,1)S(1)}, bf16[88,640]{1,0:T(8,128)(2,1)S(1)}, u32[]{:S(2)}, u32[]{:S(2)}) collective-permute-start(bf16[88,640]{1,0:T(8,128)(2,1)S(1)} %fusion.122), channel_id=1, source_target_pairs={{0,16},{4,20},{8,24},{12,28},{16,0},{20,4},{24,8},{28,12},{1,17},{... | collective-permute-start | bytes 337928 | tf_op jit(solution)/shard_map/ppermute | solution.py:35
  395.4 8.5 %collective-permute-start.17 = (bf16[352,640]{1,0:T(8,128)(2,1)S(1)}, bf16[352,640]{1,0:T(8,128)(2,1)S(1)}, u32[]{:S(2)}, u32[]{:S(2)}) collective-permute-start(bf16[352,640]{1,0:T(8,128)(2,1)S(1)} %pad_maximum_fusion.6), channel_id=1, source_target_pairs={{0,4},{4,0},{8,12},{12,8},{16,20},{20,16},{24,28},{28,24},{1,5},{5... | collective-permute-start | bytes 1351688 | tf_op jit(solution)/shard_map/ppermute | solution.py:35
  (49 other events, 590.1 us)
Sparse Core Ops, SparseCore 0:
  10.2 24.5 all-gather.3
  36.9 25.3 all-gather.5
